TPU v7x, 128 devices: a whole 4x4x4 slice. The times are simulated.
128 devices in a mesh: dp: 16 (over y_lo, z, core), mp: 8 (over y_hi, x).
Axes of the slice: x: 4, y: 4 (y_hi: 2, y_lo: 2; y = y_hi * 2 + y_lo), z: 4, core: 2. Of those that a mesh axis runs over, the one named last changes fastest.
Arguments:
- tokens: bfloat16 [16, 8, 256, 1536], P('dp', None, 'mp'), may hold values from -6 to 6
- seq_len: int32 [16], P('dp'), may hold values from 1024 to 2048, as said below
- norm_gain: float32 [1536], replicated, may hold values from 0.5 to 1.5
- main_weight: bfloat16 [1536, 2, 3072], P('dp', None, 'mp'), may hold values from -0.15625 to 0.15625
- side_weight: bfloat16 [1536, 304], P('dp'), may hold values from -0.15625 to 0.15625
- side_terms: float32 [5, 256], replicated, as said below
- channel_terms: float32 [6, 3072], P(None, 'mp'), as said below
- head_terms: float32 [3, 48], P(None, 'mp'), as said below
- output_weight: bfloat16 [3072, 1536], P('mp', 'dp'), may hold values from -0.109375 to 0.109375
- cotangent: bfloat16 [16, 8, 256, 1536], P('dp', None, 'mp'), may hold values from -6 to 6
Outputs:
- layer_out: bfloat16 [16, 8, 256, 1536], P('dp', None, 'mp')
- token_grad: float32 [16, 8, 256, 1536], P('dp', None, 'mp')
- norm_gain_grad: float32 [1536], replicated
- main_weight_grad: float32 [1536, 2, 3072], P('dp', None, 'mp')
- side_weight_grad: float32 [1536, 304], P('dp')
- side_terms_grad: float32 [5, 256], replicated
- channel_terms_grad: float32 [6, 3072], P(None, 'mp')
- head_terms_grad: float32 [3, 48], P(None, 'mp')
- output_weight_grad: float32 [3072, 1536], P('mp', 'dp')
Inputs may be any that keep to these rules, and one draw needn't show every extreme that they name: `seq_len`: lengths of the sequences; one buffer is full and one is half full in every draw. `side_terms`: taps and biases of order one. `channel_terms`: taps and biases of order one, then gains near one. `head_terms`: step biases below zero, log rates of order one, skip factors near one.
All inputs are finite; a program needn't handle non-finite values.
Results may differ from a plain program's by a relative error of at most 0.02.
Values may be sent and summed in bfloat16 or wider, within the bound.
A program may use at most 192 MiB of HBM per device.

v0:
```python
import jax
import jax.numpy as jnp
from jax import lax
from jax.sharding import PartitionSpec as P

CONV = 4
CL = 256


epsilon = 1e-05
highest = lax.Precision.HIGHEST


def causal_conv(series, terms):
    count = series.shape[0]
    padded = jnp.concatenate([jnp.zeros((CONV - 1, series.shape[1]), series.dtype), series], 0)
    total = terms[CONV] + jnp.zeros_like(series)
    for k in range(CONV):
        total = total + terms[k] * padded[k : k + count]
    return jax.nn.silu(total)


def block_step(decay, state, block):
    values, steps, keys, queries = block
    logs = jnp.cumsum(steps * decay, axis=0)
    order = jnp.arange(values.shape[0])
    lower = (order[:, None] >= order[None, :])[:, :, None]
    gaps = logs[:, None, :] - logs[None, :, :]
    weights = jnp.where(lower, jnp.exp(jnp.where(lower, gaps, 0.0)), 0.0)
    intersection = jnp.dot(queries, keys.T, precision=highest)
    mixing = weights * intersection[:, :, None] * steps[None, :, :]
    inner = jnp.einsum("tsh,shp->thp", mixing, values, precision=highest)
    carried = jnp.exp(logs)[:, :, None] * jnp.einsum(
        "tn,hpn->thp", queries, state, precision=highest
    )
    tails = jnp.exp(logs[-1][None, :] - logs) * steps
    update = jnp.einsum("sh,shp,sn->hpn", tails, values, keys, precision=highest)
    state = jnp.exp(logs[-1])[:, None, None] * state + update
    return (state, inner + carried)


def partial_step(decay):

    def stepper(state, block):
        return block_step(decay, state, block)

    return stepper


def state_scan(values, steps, decay, keys, queries, skip):
    count, heads, width = values.shape
    blocks = count // CL
    parts = (
        values.reshape(blocks, CL, heads, width),
        steps.reshape(blocks, CL, heads),
        keys.reshape(blocks, CL, -1),
        queries.reshape(blocks, CL, -1),
    )
    start = jnp.zeros((heads, width, keys.shape[1]), values.dtype)
    final, outputs = lax.scan(jax.checkpoint(partial_step(decay)), start, parts)
    return outputs.reshape(count, heads, width) + skip[None, :, None] * values


def mixer(gates, inputs, keys_raw, step_raw, side_terms, channel_terms, head_terms):
    count = inputs.shape[0]
    heads = head_terms.shape[1]
    state_size = side_terms.shape[1] // 2
    values = causal_conv(inputs, channel_terms[: CONV + 1]).reshape(count, heads, -1)
    both_keys = causal_conv(keys_raw, side_terms)
    steps = jax.nn.softplus(step_raw + head_terms[0])
    decay = -jnp.exp(head_terms[1])
    scanned = state_scan(
        values, steps, decay, both_keys[:, :state_size], both_keys[:, state_size:], head_terms[2]
    )
    return scanned.reshape(count, -1) * jax.nn.silu(gates)


def on_device(
    tokens,
    seq_len,
    norm_gain,
    main_weight,
    side_weight,
    side_terms,
    channel_terms,
    head_terms,
    output_weight,
    cotangent,
):
    stretches, piece, width = (tokens.shape[1], tokens.shape[2], tokens.shape[3])
    groups = lax.axis_size("mp")
    span = piece * groups
    count = stretches * span
    place = lax.axis_index("mp")
    heads = head_terms.shape[1]
    local_inner = channel_terms.shape[1]
    inner = local_inner * groups
    pair = 2 * side_terms.shape[1] // 2
    seq = tokens[0].astype(jnp.float32)
    scale = lax.rsqrt(jnp.mean(seq * seq, axis=-1, keepdims=True) + epsilon)
    normed = (seq * scale * norm_gain).astype(jnp.bfloat16)
    whole = lax.all_gather(normed, "mp", axis=1, tiled=True).reshape(count, width)
    main_full, side_full, out_full = (
        lax.all_gather(main_weight, "dp", axis=0, tiled=True),
        lax.all_gather(side_weight, "dp", axis=0, tiled=True),
        lax.all_gather(output_weight, "dp", axis=1, tiled=True),
    )
    both = jnp.dot(
        whole, main_full.reshape(width, 2 * local_inner), preferred_element_type=jnp.float32
    )
    small = jnp.dot(whole, side_full, preferred_element_type=jnp.float32)

    def local_mix(gates, inputs, shared, side_vals, channel_vals, head_vals):
        step_raw = lax.dynamic_slice_in_dim(shared, pair + place * heads, heads, 1)
        return mixer(gates, inputs, shared[:, :pair], step_raw, side_vals, channel_vals, head_vals)

    mixed, pull_mix = jax.vjp(
        local_mix,
        both[:, :local_inner],
        both[:, local_inner:],
        small,
        side_terms,
        channel_terms,
        head_terms,
    )
    squares = lax.psum(jnp.sum(mixed * mixed, axis=1), "mp")
    rnorm = lax.rsqrt(squares / inner + epsilon)[:, None]
    gain = channel_terms[CONV + 1]
    gated = (mixed * rnorm * gain).astype(jnp.bfloat16)
    partial_out = jnp.dot(gated, out_full, preferred_element_type=jnp.float32).reshape(
        stretches, span, width
    )
    branch = lax.psum_scatter(
        partial_out.astype(jnp.bfloat16), "mp", scatter_dimension=1, tiled=True
    ).astype(jnp.float32)
    positions = jnp.arange(stretches)[:, None] * span + place * piece + jnp.arange(piece)[None, :]
    valid = (positions < seq_len[0]).astype(jnp.float32)[:, :, None]
    result = (seq + valid * branch).astype(jnp.bfloat16)
    grad_out = cotangent[0].astype(jnp.float32)
    grad_branch = (valid * grad_out).astype(jnp.bfloat16)
    grad_full = lax.all_gather(grad_branch, "mp", axis=1, tiled=True).reshape(count, width)
    main_back, side_back, out_back = (
        lax.all_gather(main_weight, "dp", axis=0, tiled=True),
        lax.all_gather(side_weight, "dp", axis=0, tiled=True),
        lax.all_gather(output_weight, "dp", axis=1, tiled=True),
    )
    out_part = jnp.einsum("ri,rd->id", gated, grad_full, preferred_element_type=jnp.float32)
    grad_gated = jnp.einsum("rd,id->ri", grad_full, out_back, preferred_element_type=jnp.float32)
    weighted = grad_gated * gain
    products = lax.psum(jnp.sum(weighted * mixed, axis=1), "mp")
    grad_mixed = rnorm * weighted - mixed * rnorm**3 * products[:, None] / inner
    gain_part = jnp.sum(grad_gated * mixed * rnorm, axis=0)
    grad_gates, grad_inputs, grad_small, grad_side_terms, grad_channel, grad_head = pull_mix(
        grad_mixed
    )
    grad_channel = jnp.concatenate([grad_channel[: CONV + 1], gain_part[None, :]], 0)
    grad_both = jnp.concatenate([grad_gates, grad_inputs], axis=1).astype(jnp.bfloat16)
    main_part = jnp.einsum(
        "rd,rc->dc", whole, grad_both, preferred_element_type=jnp.float32
    ).reshape(width, 2, local_inner)
    norm_part = jnp.einsum(
        "rc,dc->rd",
        grad_both,
        main_back.reshape(width, 2 * local_inner),
        preferred_element_type=jnp.float32,
    )
    norm_piece, small_piece = (
        lax.psum_scatter(
            norm_part.reshape(stretches, span, width), "mp", scatter_dimension=1, tiled=True
        ),
        lax.psum_scatter(
            grad_small.reshape(stretches, span, -1), "mp", scatter_dimension=1, tiled=True
        ),
    )
    small_round = small_piece.astype(jnp.bfloat16)
    grad_normed = norm_piece + jnp.einsum(
        "cpk,dk->cpd", small_round, side_back, preferred_element_type=jnp.float32
    )
    side_part = jnp.einsum("cpd,cpk->dk", normed, small_round, preferred_element_type=jnp.float32)
    inner_sum = jnp.sum(grad_normed * norm_gain * seq, axis=-1, keepdims=True)
    token_grad = grad_out + scale * norm_gain * grad_normed - seq * scale**3 * inner_sum / width
    norm_part_gain = jnp.sum(grad_normed * seq * scale, axis=(0, 1))
    head_total, channel_total = lax.psum((grad_head, grad_channel), "dp")
    side_total = lax.psum(side_part.astype(jnp.bfloat16), "mp")
    main_grad, side_grad, out_grad = (
        lax.psum_scatter(
            main_part.astype(jnp.bfloat16), "dp", scatter_dimension=0, tiled=True
        ).astype(jnp.float32),
        lax.psum_scatter(side_total, "dp", scatter_dimension=0, tiled=True).astype(jnp.float32),
        lax.psum_scatter(
            out_part.astype(jnp.bfloat16), "dp", scatter_dimension=1, tiled=True
        ).astype(jnp.float32),
    )
    gain_total, conv_total = lax.psum((norm_part_gain, grad_side_terms), ("dp", "mp"))
    return (
        result[None],
        token_grad[None],
        gain_total,
        main_grad,
        side_grad,
        conv_total,
        channel_total,
        head_total,
        out_grad,
    )


def solution(mesh):
    placed = (
        P("dp", None, "mp", None),
        P("dp"),
        P(),
        P("dp", None, "mp"),
        P("dp", None),
        P(),
        P(None, "mp"),
        P(None, "mp"),
        P("mp", "dp"),
        P("dp", None, "mp", None),
    )
    return jax.shard_map(
        on_device,
        mesh=mesh,
        in_specs=placed,
        out_specs=(
            P("dp", None, "mp", None),
            P("dp", None, "mp", None),
            P(),
            P("dp", None, "mp"),
            P("dp", None),
            P(),
            P(None, "mp"),
            P(None, "mp"),
            P("mp", "dp"),
        ),
        check_vma=False,
    )
```

profile of v0, /device:TPU:1, one launch (start us, length us, event | category | flops | bytes accessed | tf_op | source)
XLA Modules:
  0.0 1429.5 jit_solution(5856727134860352115)
XLA Ops:
  18.2 28.1 %all_gather.19 = bf16[1536,304]{1,0:T(8,128)(2,1)S(1)} all-gather(bf16[96,304]{1,0:T(8,128)(2,1)S(1)} %copy-done.18), channel_id=1, replica_groups=mesh['dp'=16,'mp'=8] {'dp'}, dimensions={0}, use_global_device_ids=true | all-gather | bytes 992256 | tf_op jit(solution)/shard_map/all_gather | solution.py:105
  46.3 3.5 all-gather.7.cloned.1.call-done
  49.8 3.6 copy.334
  53.4 88.3 %all-gather.5.cloned.1.call-done = bf16[8,256,1536]{2,1,0:T(8,128)(2,1)} async-done(((bf16[8,32,1536]{2,1,0:T(8,128)(2,1)}), bf16[8,256,1536]{2,1,0:T(8,128)(2,1)}) %all-gather.5.cloned.1.call-update) | async-done | bytes 6291472 | tf_op jit(solution)/shard_map/all_gather | solution.py:102
  141.7 5.1 fusion.148
  150.1 5.1 fusion.149
  158.7 3.4 fusion.115
  165.1 8.5 fusion.107
  173.6 4.8 copy.248
  178.3 3.3 copy.335
  188.0 244.1 %while.44 = (s32[]{:T(128)}, f32[6,64,128]{2,1,0:T(8,128)S(1)}, f32[8,256,6,64]{1,0,3,2:T(8,128)}, f32[8,6,64,128]{3,2,1,0:T(8,128)}, f32[8,256,6]{1,2,0:T(8,128...) while((s32[]{:T(128)}, f32[6,64,128]{2,1,0:T(8,128)S(1)}, ...), condition=%wide.region_4.5_spmd.clone.clone, body=%wide.region_1.4_spmd.clone.clone.sunk | while | flops 707351040 | bytes 5768572 | solution.py:60
  189.4 3.2 reduce-window.86
  208.7 9.9 dynamic_update_slice.80
  239.3 9.9 dynamic_update_slice.80
  250.5 3.2 reduce-window.86
  269.8 9.9 dynamic_update_slice.80
  281.0 3.2 reduce-window.86
  300.3 9.9 dynamic_update_slice.80
  311.5 3.2 reduce-window.86
  330.8 9.9 dynamic_update_slice.80
  342.0 3.2 reduce-window.86
  361.3 9.9 dynamic_update_slice.80
  391.8 9.9 dynamic_update_slice.80
  422.3 9.9 dynamic_update_slice.80
  432.2 4.9 copy.336
  437.1 3.5 copy.254
  440.7 5.5 multiply_reduce_fusion.10
  446.1 16.1 %psum.49 = f32[2048]{0:T(1024)S(1)} all-reduce(f32[2048]{0:T(1024)S(1)} %get-tuple-element.858), channel_id=1, replica_groups=mesh['dp'=16,'mp'=8] {'mp'}, use_global_device_ids=true, to_apply=%region_6.7 | all-reduce | flops 2048 | bytes 16384 | tf_op jit(solution)/shard_map/psum | solution.py:126
  462.4 10.0 multiply_reduce_fusion.4
  472.3 17.0 %psum.50 = f32[2048]{0:T(1024)S(1)} all-reduce(f32[2048]{0:T(1024)S(1)} %get-tuple-element.778), channel_id=1, replica_groups=mesh['dp'=16,'mp'=8] {'mp'}, use_global_device_ids=true, to_apply=%region_9.10 | all-reduce | flops 2048 | bytes 16384 | tf_op jit(solution)/shard_map/psum | solution.py:150
  489.4 9.6 multiply_reduce_fusion.3
  507.5 293.2 %while.43 = (s32[]{:T(128)}, f32[6]{0:T(128)S(1)}, f32[6,64,128]{2,1,0:T(8,128)S(1)}, f32[8,256,6,64]{1,0,3,2:T(8,128)}, f32[8,256,6]{1,2,0:T(8,128)S(1)}, /*ind...) while((s32[]{:T(128)}, f32[6]{0:T(128)S(1)}, ...), condition=%wide.region_23.24_spmd.clone, body=%wide.region_10.23_spmd.clone.sunk | while | flops 1670427136 | bytes 14930680 | solution.py:60
  524.8 7.6 reduce-window.84
  534.5 9.8 dynamic_update_slice.78
  561.4 7.6 reduce-window.84
  571.2 9.8 dynamic_update_slice.78
  598.1 7.6 reduce-window.84
  607.8 9.8 dynamic_update_slice.78
  634.7 7.6 reduce-window.84
  644.4 9.8 dynamic_update_slice.78
  671.3 7.6 reduce-window.84
  681.1 9.8 dynamic_update_slice.78
  707.9 7.6 reduce-window.84
  717.7 9.8 dynamic_update_slice.78
  744.6 7.6 reduce-window.84
  754.3 9.8 dynamic_update_slice.78
  781.2 7.6 reduce-window.84
  790.9 9.8 dynamic_update_slice.78
  807.6 5.0 multiply_reduce_fusion.14
  818.3 3.7 copy.276
  825.2 3.5 copy.262
  828.7 8.6 convolution_convert_fusion.2
  837.3 10.5 multiply_reduce_fusion.8
  856.5 11.4 convolution_convert_fusion.1
  868.0 39.1 %reduce-scatter.11.cloned.1.call-done = f32[8,32,304]{2,1,0:T(8,128)} async-done(((f32[8,256,304]{2,1,0:T(8,128)}), f32[8,32,304]{2,1,0:T(8,128)}) %reduce-scatter.11.cloned.1.call-update) | async-done | bytes 311312 | tf_op jit(solution)/shard_map/reduce_scatter | solution.py:171
  912.7 10.3 fusion.102
  924.9 6.7 convolution_convert_fusion
  933.3 51.4 %all-reduce.29 = (f32[6,384]{1,0:T(8,128)}, f32[3,6]{1,0:T(4,128)}) all-reduce(f32[6,384]{1,0:T(8,128)S(1)} %pad_maximum_fusion, f32[3,6]{1,0:T(4,128)S(1)} %pad_add_fusion.8), channel_id=1, replica_groups=mesh['dp'=16,'mp'=8] {'dp'}, use_global_device_ids=true, to_apply=%region_44.45 | all-reduce | flops 2322 | bytes 18576 | tf_op jit(solution)/shard_map/psum | solution.py:183
  986.4 46.4 %reduce-scatter.13.cloned.1.call-done = bf16[96,2,384]{2,0,1:T(8,128)(2,1)} async-done(((bf16[1536,2,384]{2,0,1:T(8,128)(2,1)}), bf16[96,2,384]{2,0,1:T(8,128)(2,1)}) %reduce-scatter.13.cloned.1.call-update) | async-done | bytes 147472 | tf_op jit(solution)/shard_map/reduce_scatter | solution.py:186
  1034.5 61.5 %reduce-scatter.17.cloned.1.call-done = bf16[96,304]{1,0:T(8,128)(2,1)} async-done(((bf16[1536,304]{1,0:T(8,128)(2,1)}), bf16[96,304]{1,0:T(8,128)(2,1)}) %reduce-scatter.17.cloned.1.call-update) | async-done | bytes 58384 | tf_op jit(solution)/shard_map/reduce_scatter | solution.py:189
  1096.0 37.2 %psum.56 = bf16[96,304]{1,0:T(8,128)(2,1)S(1)} all-reduce(bf16[96,304]{1,0:T(8,128)(2,1)} %reduce-scatter.17.cloned.1.call-done), channel_id=1, replica_groups=mesh['dp'=16,'mp'=8] {'mp'}, use_global_device_ids=true, to_apply=%region_30.31 | all-reduce | flops 29184 | bytes 116736 | tf_op jit(solution)/shard_map/psum | solution.py:184
  1133.9 120.8 %reduce-scatter.9.cloned.1.call-done = f32[8,32,1536]{2,1,0:T(8,128)} async-done(((f32[8,256,1536]{2,1,0:T(8,128)}), f32[8,32,1536]{2,1,0:T(8,128)}) %reduce-scatter.9.cloned.1.call-update) | async-done | bytes 1572880 | tf_op jit(solution)/shard_map/reduce_scatter | solution.py:168
  1259.8 95.1 %reduce-scatter.7.cloned.1.call-done = bf16[8,32,1536]{2,1,0:T(8,128)(2,1)} async-done(((bf16[8,256,1536]{2,1,0:T(8,128)(2,1)}), bf16[8,32,1536]{2,1,0:T(8,128)(2,1)}) %reduce-scatter.7.cloned.1.call-update) | async-done | bytes 786448 | tf_op jit(solution)/shard_map/reduce_scatter | solution.py:133
  1357.5 65.0 %all-reduce.28 = (f32[1536]{0:T(1024)}, f32[5,256]{1,0:T(8,128)}) all-reduce(f32[1536]{0:T(1024)S(1)} %get-tuple-element.888, f32[5,256]{1,0:T(8,128)S(1)} %pad_add_fusion.7), channel_id=1, replica_groups=mesh['dp'=16,'mp'=8] {'dp','mp'}, use_global_device_ids=true, to_apply=%region_28.29 | all-reduce | flops 2816 | bytes 22528 | tf_op jit(solution)/shard_map/psum | solution.py:194
  (714 shorter events, 381.9 us)
Async XLA Ops:
  7.2 6.6 copy-start.17
  7.2 7.8 copy-start.61
  7.2 10.2 copy-start.58
  7.2 10.3 copy-start.50
  7.2 10.9 copy-start.18
  7.2 42.6 %all-gather.7.cloned.1.call-start = ((), (), s32[]{:S(2)}) async-start(), calls=%async_computation.7 | async-start | bytes 2506752 | tf_op jit(solution)/shard_map/all_gather | solution.py:104
  8.0 133.7 %all-gather.5.cloned.1.call-start = ((), (), s32[]{:S(2)}) async-start(), calls=%async_computation.6 | async-start | bytes 7077888 | tf_op jit(solution)/shard_map/all_gather | solution.py:102
  10.0 7.5 copy-start.20
  12.3 450.0 %all-gather.9.cloned.1.call-start = ((), (), s32[]{:S(2)}) async-start(), calls=%async_computation.8 | async-start | bytes 1253376 | tf_op jit(solution)/shard_map/all_gather | solution.py:106
  13.0 449.3 %all-gather.11.cloned.1.call-start = ((), (), s32[]{:S(2)}) async-start(), calls=%async_computation.10 | async-start | bytes 7077888 | tf_op jit(solution)/shard_map/all_gather | solution.py:141
  13.8 3.7 copy-start.22
  14.9 892.3 %reduce-scatter.11.cloned.1.call-start = ((), (), s32[]{:S(2)}) async-start(), calls=%async_computation.12 | async-start | bytes 3538944 | tf_op jit(solution)/shard_map/reduce_scatter | solution.py:171
  17.5 141.2 %copy-start.34 = (f32[1,256]{1,0:T(1,128)}, f32[1,256]{1,0:T(1,128)S(1)}, u32[]{:S(2)}) copy-start(f32[1,256]{1,0:T(1,128)S(1)} %get-tuple-element.893) | copy-start | bytes 3076
  17.5 141.2 %copy-start.36 = (f32[1,256]{1,0:T(1,128)}, f32[1,256]{1,0:T(1,128)S(1)}, u32[]{:S(2)}) copy-start(f32[1,256]{1,0:T(1,128)S(1)} %get-tuple-element.894) | copy-start | bytes 3076
  17.5 141.2 %copy-start.38 = (f32[1,256]{1,0:T(1,128)}, f32[1,256]{1,0:T(1,128)S(1)}, u32[]{:S(2)}) copy-start(f32[1,256]{1,0:T(1,128)S(1)} %get-tuple-element.895) | copy-start | bytes 3076
  17.5 141.2 %copy-start.40 = (f32[1,256]{1,0:T(1,128)}, f32[1,256]{1,0:T(1,128)S(1)}, u32[]{:S(2)}) copy-start(f32[1,256]{1,0:T(1,128)S(1)} %get-tuple-element.896) | copy-start | bytes 3076
  18.1 146.9 %copy-start.25 = (f32[384]{0:T(512)}, f32[384]{0:T(512)S(1)}, u32[]{:S(2)}) copy-start(f32[384]{0:T(512)S(1)} %get-tuple-element.793) | copy-start | bytes 4612
  18.1 146.9 %copy-start.27 = (f32[384]{0:T(512)}, f32[384]{0:T(512)S(1)}, u32[]{:S(2)}) copy-start(f32[384]{0:T(512)S(1)} %get-tuple-element.794) | copy-start | bytes 4612
  18.1 146.9 %copy-start.29 = (f32[384]{0:T(512)}, f32[384]{0:T(512)S(1)}, u32[]{:S(2)}) copy-start(f32[384]{0:T(512)S(1)} %get-tuple-element.795) | copy-start | bytes 4612
  18.2 146.9 %copy-start.31 = (f32[384]{0:T(512)}, f32[384]{0:T(512)S(1)}, u32[]{:S(2)}) copy-start(f32[384]{0:T(512)S(1)} %get-tuple-element.797) | copy-start | bytes 4612
  46.3 100.5 %copy-start.12 = (bf16[1536,304]{1,0:T(8,128)(2,1)}, bf16[1536,304]{1,0:T(8,128)(2,1)S(1)}, u32[]{:S(2)}) copy-start(bf16[1536,304]{1,0:T(8,128)(2,1)S(1)} %all_gather.19) | copy-start | bytes 2801668
  141.6 5.3 copy-start.62
  146.7 8.4 copy-start.8
  146.7 3.3 copy-start.16
  147.0 11.7 copy-start.3
  155.1 3.6 copy-start.2
  173.6 315.8 %copy-start = (f32[2048,384]{1,0:T(8,128)}, f32[2048,384]{1,0:T(8,128)S(1)}, u32[]{:S(2)}) copy-start(f32[2048,384]{1,0:T(8,128)S(1)} %get-tuple-element.863) | copy-start | bytes 9437188
  181.6 2.7 copy-start.51
  437.1 3.5 copy-start.24
  440.7 21.7 %copy-start.48 = (f32[384]{0:T(512)S(1)}, f32[384]{0:T(512)}, u32[]{:S(2)}) copy-start(f32[384]{0:T(512)} %get-tuple-element.792) | copy-start | bytes 4612
  504.4 3.1 copy-start.19
  504.4 3.1 copy-start.33
  507.5 295.8 %copy-start.52 = (f32[6]{0:T(128)S(1)}, f32[6]{0:T(128)}, u32[]{:S(2)}) copy-start(f32[6]{0:T(128)} %get-tuple-element.900) | copy-start | bytes 76
  800.7 6.8 copy-start.4
  807.6 5.0 copy-start.35
  807.6 5.0 copy-start.37
  807.6 5.0 copy-start.39
  807.6 5.0 copy-start.41
  818.3 3.7 copy-start.6
  821.9 162.9 %reduce-scatter.15.cloned.1.call-start = ((), (), s32[]{:S(2)}) async-start(), calls=%async_computation.14 | async-start | bytes 1253376 | tf_op jit(solution)/shard_map/reduce_scatter | solution.py:190
  825.2 3.5 copy-start.49
  828.7 8.6 copy-start.1
  837.3 11.0 copy-start.26
  837.3 11.0 copy-start.28
  837.3 11.0 copy-start.30
  837.3 11.1 copy-start.32
  847.9 184.9 %reduce-scatter.13.cloned.1.call-start = ((), (), s32[]{:S(2)}) async-start(), calls=%async_computation.13 | async-start | bytes 2506752 | tf_op jit(solution)/shard_map/reduce_scatter | solution.py:186
  851.1 2.1 copy-start.10
  856.5 50.7 %copy-start.15 = (bf16[8,32,1536]{2,1,0:T(8,128)(2,1)S(1)}, bf16[8,32,1536]{2,1,0:T(8,128)(2,1)}, u32[]{:S(2)}) copy-start(bf16[8,32,1536]{2,1,0:T(8,128)(2,1)} %fusion.119) | copy-start | bytes 2359300
  868.0 41.9 %copy-start.7 = (bf16[1536,2,384]{2,1,0:T(2,128)(2,1)S(1)}, bf16[1536,2,384]{2,1,0:T(2,128)(2,1)}, u32[]{:S(2)}) copy-start(bf16[1536,2,384]{2,1,0:T(2,128)(2,1)} %all-gather.7.cloned.1.call-done) | copy-start | bytes 7077892
  868.0 228.0 %reduce-scatter.17.cloned.1.call-start = ((), (), s32[]{:S(2)}) async-start(), calls=%async_computation.15 | async-start | bytes 1253376 | tf_op jit(solution)/shard_map/reduce_scatter | solution.py:189
  909.8 344.8 %reduce-scatter.9.cloned.1.call-start = ((), (), s32[]{:S(2)}) async-start(), calls=%async_computation.11 | async-start | bytes 14155776 | tf_op jit(solution)/shard_map/reduce_scatter | solution.py:168
  923.0 1.9 copy-start.5
  923.1 431.9 %reduce-scatter.7.cloned.1.call-start = ((), (), s32[]{:S(2)}) async-start(), calls=%async_computation.9 | async-start | bytes 7077888 | tf_op jit(solution)/shard_map/reduce_scatter | solution.py:133
  931.6 1.6 copy-start.59
  931.7 53.1 %copy-start.53 = (f32[256]{0:T(256)S(1)}, f32[256]{0:T(256)}, u32[]{:S(2)}) copy-start(f32[256]{0:T(256)} %get-tuple-element.787) | copy-start | bytes 3076
  931.7 53.1 %copy-start.54 = (f32[256]{0:T(256)S(1)}, f32[256]{0:T(256)}, u32[]{:S(2)}) copy-start(f32[256]{0:T(256)} %get-tuple-element.788) | copy-start | bytes 3076
  931.7 53.1 %copy-start.55 = (f32[256]{0:T(256)S(1)}, f32[256]{0:T(256)}, u32[]{:S(2)}) copy-start(f32[256]{0:T(256)} %get-tuple-element.789) | copy-start | bytes 3076
  931.7 53.1 %copy-start.56 = (f32[256]{0:T(256)S(1)}, f32[256]{0:T(256)}, u32[]{:S(2)}) copy-start(f32[256]{0:T(256)} %get-tuple-element.790) | copy-start | bytes 3076
  931.7 53.1 %copy-start.57 = (f32[256]{0:T(256)S(1)}, f32[256]{0:T(256)}, u32[]{:S(2)}) copy-start(f32[256]{0:T(256)} %get-tuple-element.791) | copy-start | bytes 3076
  931.7 323.0 %copy-start.13 = (bf16[1536,304]{1,0:T(8,128)(2,1)S(1)}, bf16[1536,304]{1,0:T(8,128)(2,1)}, u32[]{:S(2)}) copy-start(bf16[1536,304]{1,0:T(8,128)(2,1)} %copy-done.12) | copy-start | bytes 2801668
  931.7 325.1 %copy-start.9 = (bf16[1,8,32,1536]{3,2,1,0:T(8,128)(2,1)S(1)}, bf16[1,8,32,1536]{3,2,1,0:T(8,128)(2,1)}, u32[]{:S(2)}) copy-start(bf16[1,8,32,1536]{3,2,1,0:T(8,128)(2,1)} %param.14) | copy-start | bytes 2359300
  931.7 325.1 %copy-start.21 = (f32[8,32]{1,0:T(8,128)S(1)}, f32[8,32]{1,0:T(8,128)}, u32[]{:S(2)}) copy-start(f32[8,32]{1,0:T(8,128)} %copy-done.20) | copy-start | bytes 3076
  1256.8 98.1 %copy-start.23 = (f32[8,32]{1,0:T(8,128)S(1)}, f32[8,32]{1,0:T(8,128)}, u32[]{:S(2)}) copy-start(f32[8,32]{1,0:T(8,128)} %copy-done.22) | copy-start | bytes 3076
  (9 other events, 7.4 us)
Sparse Core Ops, SparseCore 0:
  9.8 39.9 all-gather.6
  52.6 88.9 all-gather.4
  143.4 31.5 all-gather.8
  177.1 88.7 all-gather.10
  822.1 85.0 reduce-scatter.10
  909.6 58.3 reduce-scatter.14
  970.5 62.2 reduce-scatter.12
  1035.3 60.6 reduce-scatter.16
  1100.4 154.2 reduce-scatter.8
  1258.4 96.4 reduce-scatter.6
where the time goes:
time: 1440 us; the launch traced here: 1430 us
  waiting for transfers between devices  456 us (32%)
  local copies, waits for them, and re-layouts  340 us (24%)
  blocking collectives  215 us (15%)
  other arithmetic  206 us (14%)
  matrix products  194 us (13%)
  between operations  15.8 us (1%)
    dynamic_update_slice x32, local copies, waits for them, and re-layouts, state_scan(): final, outputs = lax.scan(jax.checkpoint(partial_step(decay)), start, parts)  170 us
    reduce_scatter x1, waiting for transfers between devices, on_device(): lax.psum_scatter(norm_part.reshape(stretches, span, width), 'mp', scatter...  121 us
    another operation x73, other arithmetic  120 us
    reduce_scatter x1, waiting for transfers between devices, on_device(): lax.psum_scatter(partial_out.astype(jnp.bfloat16), 'mp', scatter_dimensio...  95.1 us
    all_gather x1, waiting for transfers between devices, on_device(): lax.all_gather(normed, 'mp', axis=1, tiled=True).reshape(count, width)  88.3 us
    psum x1, blocking collectives, on_device(): lax.psum((norm_part_gain, grad_side_terms), ('dp', 'mp'))  65 us
    reduce_scatter x1, waiting for transfers between devices, on_device(): lax.psum_scatter(side_total, 'dp', scatter_dimension=0, tiled=True)  61.5 us
    dot_general x24, matrix products, block_step(): inner = jnp.einsum('tsh,shp->thp', mixing, values, precision=highest)  56.5 us
  transfers between devices with their start and end apart: 10, of which 7 were waited for; matrix products, arithmetic and copies ran while one was open for 27% of the time, Pallas kernels for 0%

commit v1 on v0

v1 whole, which is shorter than its diff:
```python
import functools

import jax
import jax.numpy as jnp
from jax import lax
from jax.experimental import pallas as pl
from jax.experimental.pallas import tpu as pltpu
from jax.sharding import PartitionSpec as P

f32, bf16 = jnp.float32, jnp.bfloat16
CONV, D, INNER = 4, 1536, 3072
L, N, PW, IN, HD = 256, 128, 64, 384, 6
BLOCKS, GROUP, PIECE, DP = 8, 8, 32, 16
COLS = 2 * IN + 3 * N
MIX = IN + 2 * N
MESH = pl.DeviceIdType.MESH
VMEM_BYTES = 60 * 2**20
epsilon = 1e-05
NEG = -1e30

def mm(a, b):
    return lax.dot_general(a, b, (((1,), (0,)), ((), ())), preferred_element_type=f32)
def mm_nt(a, b):
    return lax.dot_general(a, b, (((1,), (1,)), ((), ())), preferred_element_type=f32)
def mm_tn(a, b):
    return lax.dot_general(a, b, (((0,), (0,)), ((), ())), preferred_element_type=f32)

def thirds(x):
    hi = x.astype(bf16)
    rest = x - hi.astype(f32)
    mid = rest.astype(bf16)
    return hi, mid, (rest - mid.astype(f32)).astype(bf16)

def exact_left(mask, x):
    a, b, c = thirds(x)
    return mm(mask, a) + mm(mask, b) + mm(mask, c)

def exact_right(x, mask):
    a, b, c = thirds(x)
    return mm(a, mask) + mm(b, mask) + mm(c, mask)

def sigmoid(x):
    return 1.0 / (1.0 + jnp.exp(-x))

def softplus(x):
    return jnp.maximum(x, 0.0) + jnp.log1p(jnp.exp(-jnp.abs(x)))

def tri(lower):
    r = lax.broadcasted_iota(jnp.int32, (L, L), 0)
    c = lax.broadcasted_iota(jnp.int32, (L, L), 1)
    return jnp.where((r >= c) if lower else (r <= c), 1.0, 0.0).astype(bf16)

def spread(cols, low):
    out = []
    for j in range(3):
        a = jnp.broadcast_to(cols[:, 2 * j : 2 * j + 1], (cols.shape[0], 128))
        b = jnp.broadcast_to(cols[:, 2 * j + 1 : 2 * j + 2], (cols.shape[0], 128))
        out.append(jnp.where(low, a, b))
    return jnp.concatenate(out, 1)

def conv_pre(window, taps):
    total = taps[4:5]
    for k in range(4):
        total = total + taps[k : k + 1] * window[5 + k : 5 + k + L]
    return total

def low_lanes(rows):
    return lax.broadcasted_iota(jnp.int32, (rows, 128), 1) < 64

def head_quantities(dt_raw, heads):
    pre = dt_raw + heads[0:1]
    dt = softplus(pre)
    logs = exact_left(tri(True), dt * heads[1:2])
    return pre, dt, logs

def half_mask(t):
    rows = 128
    r = lax.broadcasted_iota(jnp.int32, (rows, 128 * (t + 1)), 0) + 128 * t
    c = lax.broadcasted_iota(jnp.int32, (rows, 128 * (t + 1)), 1)
    return r >= c

def weights_of(logs, logs_t, h, t):
    w = 128 * (t + 1)
    col = jnp.broadcast_to(logs[128 * t : 128 * (t + 1), h : h + 1], (128, 128))
    if t:
        col = jnp.concatenate([col, col], 1)
    gap = col - logs_t[h : h + 1, :w]
    return jnp.exp(jnp.where(half_mask(t), gap, NEG))

def fwd_block(window, gates, dt_raw, taps, heads, skip, state):
    low = low_lanes(L)
    total = conv_pre(window, taps)
    act = total * sigmoid(total)
    x, b, c = act[:, :IN], act[:, IN : IN + N].astype(bf16), act[:, IN + N :].astype(bf16)
    pre, dt, logs = head_quantities(dt_raw, heads)
    logs_t = logs.T
    dt_l, logs_l = spread(dt, low), spread(logs, low)
    xd = (dt_l * x).astype(bf16)
    g = mm_nt(c, b)
    half_low = low_lanes(128)
    rows = [[], []]
    zero = jnp.zeros((), bf16)
    for j in range(3):
        pair = xd[:, 128 * j : 128 * (j + 1)]
        own = (jnp.where(low, pair, zero), jnp.where(low, zero, pair))
        for t in range(2):
            w = 128 * (t + 1)
            total_y = 0.0
            for e in range(2):
                m = weights_of(logs, logs_t, 2 * j + e, t) * g[128 * t : 128 * (t + 1), :w]
                total_y = total_y + mm(m.astype(bf16), own[e][:w])
            rows[t].append(total_y)
    intra = jnp.concatenate([jnp.concatenate(r, 1) for r in rows], 0)
    scan = intra + jnp.exp(logs_l) * mm(c, state.astype(bf16))
    last = logs_l[L - 1 : L]
    tails = jnp.exp(last - logs_l)
    state = jnp.exp(last) * state + mm_tn(b, (tails * xd.astype(f32)).astype(bf16))
    mixed = (scan + skip * x) * (gates * sigmoid(gates))
    return scan, mixed, state

def bwd_block(window, gates, dt_raw, taps, heads, skip, gain, state, state_next, scan, rnorm, products, g_gated, d_state, after):
    low = low_lanes(L)
    total = conv_pre(window, taps)
    sig = sigmoid(total)
    act = total * sig
    d_act = sig + act * (1.0 - sig)
    x, b, c = act[:, :IN], act[:, IN : IN + N].astype(bf16), act[:, IN + N :].astype(bf16)
    pre, dt, logs = head_quantities(dt_raw, heads)
    logs_t = logs.T
    dt_l, logs_l = spread(dt, low), spread(logs, low)
    xd = (dt_l * x).astype(bf16)
    xdf = xd.astype(f32)
    gsig = sigmoid(gates)
    gate = gates * gsig
    y = scan + skip * x
    mixed = y * gate
    g_mixed = rnorm * (g_gated * gain) - mixed * (rnorm * rnorm * rnorm * products * (1.0 / 3072.0))
    gain_sum = jnp.sum(g_gated * mixed * rnorm, axis=0, keepdims=True)
    dy = g_mixed * gate
    d_gates = g_mixed * y * (gsig + gate * (1.0 - gsig))
    skip_sum = jnp.sum(dy * x, axis=0, keepdims=True)
    dyb = dy.astype(bf16)
    g = mm_nt(c, b)
    zero = jnp.zeros((), bf16)
    dg = [0.0, 0.0]
    parts = []
    for j in range(3):
        pair_x = xd[:, 128 * j : 128 * (j + 1)]
        pair_y = dyb[:, 128 * j : 128 * (j + 1)]
        own = (jnp.where(low, pair_y, zero), jnp.where(low, zero, pair_y))
        upper, lower = 0.0, 0.0
        for e in range(2):
            for t in range(2):
                w = 128 * (t + 1)
                wt = weights_of(logs, logs_t, 2 * j + e, t)
                mine = own[e][128 * t : 128 * (t + 1)]
                dm = mm_nt(mine, pair_x[:w])
                dg[t] = dg[t] + dm * wt
                m = (wt * g[128 * t : 128 * (t + 1), :w]).astype(bf16)
                back = mm_tn(m, mine)
                upper = upper + back[:128]
                if t:
                    lower = lower + back[128:]
        parts.append(jnp.concatenate([upper, lower], 0))
    d_intra = jnp.concatenate(parts, 1)
    e_l = jnp.exp(logs_l)
    last = logs_l[L - 1 : L]
    tails = jnp.exp(last - logs_l)
    sb = state.astype(bf16)
    dsb = d_state.astype(bf16)
    edy = (e_l * dy).astype(bf16)
    txd = (tails * xdf).astype(bf16)
    v = mm(b, dsb)
    dxd = d_intra + tails * v
    dg0, dg1 = dg[0].astype(bf16), dg[1].astype(bf16)
    dc = mm_nt(edy, sb) + jnp.concatenate([mm(dg0, b[:128]), mm(dg1, b)], 0)
    first = mm_tn(dg0, c[:128])
    second = mm_tn(dg1, c[128:])
    db = mm_nt(txd, dsb) + jnp.concatenate([first + second[:128], second[128:]], 0)
    z = dyb.astype(f32) * scan - xdf * d_intra - txd.astype(f32) * v
    boundary = jnp.sum(state_next * dsb.astype(f32), axis=0, keepdims=True)
    row = lax.broadcasted_iota(jnp.int32, (L, IN), 0)
    z = jnp.where(row == L - 1, z + boundary, z)
    r = lax.broadcasted_iota(jnp.int32, (IN, 128), 0)
    cc = lax.broadcasted_iota(jnp.int32, (IN, 128), 1)
    fold = jnp.where((r // PW) == cc, 1.0, 0.0).astype(bf16)
    dl = exact_right(z, fold)
    g_adt = exact_left(tri(False), dl)
    direct = exact_right(x * dxd, fold)
    d_pre = (direct + heads[1:2] * g_adt) * sigmoid(pre)
    decay_sum = jnp.sum(dt * g_adt, axis=0, keepdims=True)
    bias_sum = jnp.sum(d_pre, axis=0, keepdims=True)
    d_state = jnp.exp(last) * d_state + mm_tn(c, edy)
    dx = dt_l * dxd + skip * dy
    g_pre = jnp.concatenate([dx, db, dc], 1) * d_act
    longer = jnp.concatenate([g_pre, after], 0)
    d_raw = 0.0
    tap_sums = []
    for k in range(4):
        d_raw = d_raw + taps[k : k + 1] * longer[3 - k : 3 - k + L]
        tap_sums.append(jnp.sum(g_pre * window[5 + k : 5 + k + L], axis=0, keepdims=True))
    tap_sums.append(jnp.sum(g_pre, axis=0, keepdims=True))
    g_all = jnp.concatenate([d_gates.astype(bf16), d_raw.astype(bf16), d_pre.astype(bf16)], 1)
    return g_all, d_state, g_pre[:8], (jnp.concatenate(tap_sums, 0), gain_sum, skip_sum, decay_sum, bias_sum)


class Place:
    def __init__(self):
        self.dp, self.mp = lax.axis_index("dp"), lax.axis_index("mp")
        self.hi, self.x = self.mp // 4, self.mp % 4
        self.ylo, self.z, self.core = self.dp // 8, (self.dp // 2) % 4, self.dp % 2
        self.right = (self.dp, self.hi * 4 + (self.x + 1) % 4)
        self.left = (self.dp, self.hi * 4 + (self.x + 3) % 4)
        self.across = (self.dp, (1 - self.hi) * 4 + self.x)
        self.mate = (self.dp + 1 - 2 * self.core, self.mp)
        self.beside = (self.at(1 - self.ylo, self.z, self.core), self.mp)
        self.along = [(self.at(self.ylo, (self.z + k) % 4, self.core), self.mp) for k in (1, 2, 3)]
        self.group = [(self.dp, (self.mp + k) % GROUP) for k in range(1, GROUP)]
        self.copies = [((self.dp + k) % DP, self.mp) for k in range(1, DP)]

    def at(self, ylo, z, core):
        return ylo * 8 + z * 2 + core


def meet(peers):
    barrier = pltpu.get_barrier_semaphore()
    for peer in peers:
        pl.semaphore_signal(barrier, inc=1, device_id=peer, device_id_type=MESH)
    pl.semaphore_wait(barrier, len(peers))


class Sender:
    def __init__(self, send_sem, recv_sem):
        self.send_sem, self.recv_sem, self.count, self.started = send_sem, recv_sem, 0, []

    def __call__(self, source, target, peer):
        k = self.count
        self.count += 1
        copy = pltpu.make_async_remote_copy(
            src_ref=source,
            dst_ref=target,
            send_sem=self.send_sem.at[k],
            recv_sem=self.recv_sem.at[k],
            device_id=peer,
            device_id_type=MESH,
        )
        copy.start()
        self.started.append(copy)
        return copy

    def drain(self):
        for copy in self.started:
            copy.wait_send()


def gather_steps(send, place, buf):
    hi, x, me = place.hi, place.x, place.mp
    lx, rx, ox = hi * 4 + (x + 3) % 4, hi * 4 + (x + 1) % 4, hi * 4 + (x + 2) % 4
    flip = (1 - hi) * 4
    lxy, rxy, ym = flip + (x + 3) % 4, flip + (x + 1) % 4, flip + x
    right, left, across = place.right, place.left, place.across

    def go(slot, g, h, to):
        part = buf.at[pl.ds(4 * g + 2 * h, 2), slot]
        return send(part, part, to)

    c = [go(me, 1, 0, across), go(me, 1, 1, across)]
    a = [go(me, 0, 0, right), go(me, 0, 1, left), go(me, 0, 1, right), go(me, 0, 0, left)]
    b = [go(me, 1, 0, right), go(me, 1, 1, left), go(me, 1, 1, right), go(me, 1, 0, left)]
    y = [go(me, 0, 0, across), go(me, 0, 1, across)]
    yield
    a[0].wait_recv()
    f = [go(lx, 0, 0, right)]
    y.append(go(lx, 0, 0, across))
    a[1].wait_recv()
    f.append(go(rx, 0, 1, left))
    y.append(go(rx, 0, 1, across))
    yield
    a[2].wait_recv()
    y.append(go(lx, 0, 1, across))
    a[3].wait_recv()
    y.append(go(rx, 0, 0, across))
    yield
    b[0].wait_recv()
    k = [go(lx, 1, 0, right)]
    b[1].wait_recv()
    k.append(go(rx, 1, 1, left))
    c[0].wait_recv()
    c[1].wait_recv()
    d = [go(ym, 1, 0, right), go(ym, 1, 1, left), go(ym, 1, 1, right), go(ym, 1, 0, left)]
    yield
    f[0].wait_recv()
    y.append(go(ox, 0, 0, across))
    f[1].wait_recv()
    y.append(go(ox, 0, 1, across))
    yield
    d[0].wait_recv()
    e = [go(lxy, 1, 0, right)]
    d[1].wait_recv()
    e.append(go(rxy, 1, 1, left))
    yield
    for copy in [b[2], b[3], d[2], d[3]] + k + e + y:
        copy.wait_recv()


def weight_steps(send, place, buf):
    own, other = place.dp, place.at(1 - place.ylo, place.z, place.core)
    one = send(buf.at[own], buf.at[own], place.beside)
    mates = [send(buf.at[own], buf.at[own], place.mate)]
    near = [send(buf.at[own], buf.at[own], peer) for peer in place.along]
    yield
    one.wait_recv()
    mates.append(send(buf.at[other], buf.at[other], place.mate))
    far = [send(buf.at[other], buf.at[other], peer) for peer in place.along]
    yield
    for k in range(3):
        near[k].wait_recv()
        slot = place.at(place.ylo, (place.z + 3 - k) % 4, place.core)
        mates.append(send(buf.at[slot], buf.at[slot], place.mate))
    yield
    for k in range(3):
        far[k].wait_recv()
        slot = place.at(1 - place.ylo, (place.z + 3 - k) % 4, place.core)
        mates.append(send(buf.at[slot], buf.at[slot], place.mate))
    yield
    for copy in mates:
        copy.wait_recv()


def add_into(buf, first, slot, other, where, count):
    def body(i, carry):
        total = buf[first + i, slot].astype(f32) + other[where(i)].astype(f32)
        buf[first + i, slot] = total.astype(bf16)
        return carry

    lax.fori_loop(0, count, body, 0)


def scatter_steps(send, place, buf, y_in, x_in, xx_in, t_out, t_in, total):
    hi, x = place.hi, place.x
    right, left, across = place.right, place.left, place.across
    order = [(x + 2) % 4, (x + 1) % 4, (x + 3) % 4, x]
    mine, theirs = hi * 4, (1 - hi) * 4

    def first_hop(k, base, side):
        slot = side + order[0]
        return [
            send(buf.at[pl.ds(base, 2), slot], x_in.at[k, 0], right),
            send(buf.at[pl.ds(base + 2, 2), slot], x_in.at[k, 1], left),
        ]

    def second_hop(k, base, side, hops):
        hops[0].wait_recv()
        add_into(buf, base, side + order[1], x_in, lambda i: (k, 0, i), 2)
        one = send(buf.at[pl.ds(base, 4), side + order[1]], xx_in.at[k, 0], right)
        hops[1].wait_recv()
        add_into(buf, base + 2, side + order[2], x_in, lambda i: (k, 1, i), 2)
        return [one, send(buf.at[pl.ds(base, 4), side + order[2]], xx_in.at[k, 1], left)]

    def three(k, base, side, i):
        return (
            buf[base + i, side + x].astype(f32)
            + xx_in[k, 0, i].astype(f32)
            + xx_in[k, 1, i].astype(f32)
        )

    ahead = []
    for k in range(4):
        ahead.append(send(buf.at[pl.ds(0, 4), theirs + order[k]], y_in.at[k], across))
    hop_t = first_hop(1, 4, theirs)
    hop_m = first_hop(2, 4, mine)
    yield
    two_t = second_hop(1, 4, theirs, hop_t)
    yield
    ahead[0].wait_recv()
    add_into(buf, 0, mine + order[0], y_in, lambda i: (0, i), 4)
    hop_a = first_hop(0, 0, mine)
    two_m = second_hop(2, 4, mine, hop_m)
    yield
    for copy in two_t:
        copy.wait_recv()

    def give(i, carry):
        t_out[i] = three(1, 4, theirs, i).astype(bf16)
        return carry

    lax.fori_loop(0, 4, give, 0)
    last = send(t_out, t_in, across)
    yield
    for k in range(1, 4):
        ahead[k].wait_recv()
        add_into(buf, 0, mine + order[k], y_in, lambda i, k=k: (k, i), 4)
    two_a = second_hop(0, 0, mine, hop_a)
    yield
    for copy in two_m + [last]:
        copy.wait_recv()

    def keep_b(i, carry):
        total[4 + i] = three(2, 4, mine, i) + t_in[i].astype(f32)
        return carry

    lax.fori_loop(0, 4, keep_b, 0)
    yield
    for copy in two_a:
        copy.wait_recv()

    def keep_a(i, carry):
        total[i] = three(0, 0, mine, i)
        return carry

    lax.fori_loop(0, 4, keep_a, 0)


SCATTER_SCRATCH = [
    pltpu.VMEM((4, 4, PIECE, D), bf16),
    pltpu.VMEM((3, 2, 2, PIECE, D), bf16),
    pltpu.VMEM((3, 2, 4, PIECE, D), bf16),
    pltpu.VMEM((4, PIECE, D), bf16),
    pltpu.VMEM((4, PIECE, D), bf16),
]


def finish(steps):
    for _ in steps:
        pass


def rows(block, count=L):
    return pl.ds(pl.multiple_of(block * count, count), count)


def pick(columns, block):
    lane = lax.broadcasted_iota(jnp.int32, columns.shape, 1)
    return jnp.sum(jnp.where(lane == block, columns, 0.0), axis=1, keepdims=True)


def gather_kernel(normed, weights, grad, whole, full, back, send_sem, recv_sem, local_sem):
    place = Place()
    own = [
        pltpu.make_async_copy(normed, whole.at[:, place.mp], local_sem.at[0]),
        pltpu.make_async_copy(weights, full.at[place.dp], local_sem.at[1]),
        pltpu.make_async_copy(grad, back.at[:, place.mp], local_sem.at[2]),
    ]
    for copy in own:
        copy.start()
    meet([place.right, place.left, place.across, place.mate, place.beside] + place.along)
    for copy in own:
        copy.wait()
    send = Sender(send_sem, recv_sem)
    plans = [gather_steps(send, place, whole), weight_steps(send, place, full)]
    for _ in range(2):
        for plan in plans:
            next(plan)
    for plan in plans:
        finish(plan)
    finish(gather_steps(send, place, back))
    send.drain()


def forward_kernel(
    whole, weights, back, taps, heads, skip, gain,
    raw, gates, steps, scan, mixed, states, g_gated, sums,
    squares, state, inbox, send_sem, recv_sem,
):
    place = Place()
    meet(place.group)
    raw[pl.ds(0, 8)] = jnp.zeros((8, MIX), f32)
    state[...] = jnp.zeros((N, IN), f32)
    squares[...] = jnp.zeros((L, 128), f32)
    lane = lax.broadcasted_iota(jnp.int32, (L, 128), 1)

    def body(i, carry):
        at = rows(i)
        both = mm(whole[at], weights[:, :COLS])
        gates[at] = both[:, :IN]
        steps[at] = both[:, IN + MIX :]
        raw[pl.ds(pl.multiple_of(i * L + 8, 8), L)] = both[:, IN : IN + MIX]
        states[i] = state[...]
        window = raw[pl.ds(pl.multiple_of(i * L, 8), L + 8)]
        inner, out, after = fwd_block(
            window, gates[at], steps[at], taps[...], heads[...], skip[...], state[...]
        )
        scan[at] = inner
        mixed[at] = out
        state[...] = after
        back_out = mm(back[at], weights[:, COLS:])
        g_gated[at] = back_out
        square = jnp.sum(out * out, axis=1, keepdims=True)
        product = jnp.sum(back_out * gain[...] * out, axis=1, keepdims=True)
        kept = squares[...]
        squares[...] = jnp.where(lane == i, square, jnp.where(lane == i + 8, product, kept))
        return carry

    lax.fori_loop(0, BLOCKS, body, 0)
    states[BLOCKS] = state[...]
    inbox[place.mp] = squares[...].T[:16]
    send = Sender(send_sem, recv_sem)
    copies = [send(inbox.at[place.mp], inbox.at[place.mp], peer) for peer in place.group]
    for copy in copies:
        copy.wait_recv()
    send.drain()
    total = inbox[0]
    for k in range(1, GROUP):
        total = total + inbox[k]
    top = lax.rsqrt(total[:8] * (1.0 / INNER) + epsilon)
    sums[...] = jnp.concatenate([top, total[8:], jnp.zeros((112, L), f32)], 0).T


def backward_kernel(
    raw, gates, steps, scan, mixed, states, g_gated, sums, weights, taps, heads, skip, gain,
    g_all, gated, branch, totals,
    parts, y_in, x_in, xx_in, t_out, t_in, d_state, after, send_sem, recv_sem,
):
    place = Place()
    meet([place.right, place.left, place.across])

    def spread_out(i, carry):
        at = rows(i)
        scale = pick(sums[...], i)
        rounded = (mixed[at] * scale * gain[...]).astype(bf16)
        gated[at] = rounded
        parts[i] = mm_nt(rounded, weights[:, COLS:]).astype(bf16).reshape(GROUP, PIECE, D)
        return carry

    lax.fori_loop(0, BLOCKS, spread_out, 0)
    send = Sender(send_sem, recv_sem)
    plan = scatter_steps(send, place, parts, y_in, x_in, xx_in, t_out, t_in, branch)
    next(plan)
    d_state[...] = jnp.zeros((N, IN), f32)
    after[...] = jnp.zeros((8, MIX), f32)
    totals[...] = jnp.zeros((16, MIX), f32)

    def body(j, carry):
        i = BLOCKS - 1 - j
        at = rows(i)
        window = raw[pl.ds(pl.multiple_of(i * L, 8), L + 8)]
        g, ds, top, found = bwd_block(
            window, gates[at], steps[at], taps[...], heads[...], skip[...], gain[...],
            states[i], states[i + 1], scan[at], pick(sums[...], i), pick(sums[...], i + 8),
            g_gated[at], d_state[...], after[...],
        )
        g_all[at] = g
        d_state[...] = ds
        after[...] = top
        tap_sums, gain_sum, skip_sum, decay_sum, bias_sum = found
        blank = jnp.zeros((1, MIX - IN), f32)
        fill = jnp.zeros((1, MIX - 2 * N), f32)
        totals[...] += jnp.concatenate(
            [
                tap_sums,
                jnp.concatenate([gain_sum, blank], 1),
                jnp.concatenate([skip_sum, blank], 1),
                jnp.concatenate([decay_sum, bias_sum, fill], 1),
                jnp.zeros((8, MIX), f32),
            ],
            0,
        )
        return carry

    run_between(body, plan)
    finish(plan)
    send.drain()


def run_between(body, plan):
    lax.fori_loop(0, BLOCKS, body, 0)


def last_kernel(
    whole, back, gated, g_all, weights, tokens, scale, grad_out, norm_gain, totals,
    token_grad, gain_grad, mine_grad, side_grad, shared_sums, copy_sums,
    parts, y_in, x_in, xx_in, t_out, t_in, summed, grads, core_in, z_in, y_out, w_in,
    inbox, side_box, sums_box, gain_box, gain_all, send_sem, recv_sem,
):
    place = Place()
    meet(place.group + place.copies)
    send = Sender(send_sem, recv_sem)

    sums_box[place.dp] = totals[...]
    early = [send(sums_box.at[place.dp], sums_box.at[place.dp], peer) for peer in place.copies]

    def spread_out(i, carry):
        at = rows(i)
        parts[i] = mm_nt(g_all[at], weights[:, :COLS]).astype(bf16).reshape(GROUP, PIECE, D)
        return carry

    lax.fori_loop(0, BLOCKS, spread_out, 0)
    plan = scatter_steps(send, place, parts, y_in, x_in, xx_in, t_out, t_in, summed)
    next(plan)

    def product(i, carry):
        lanes = pl.ds(pl.multiple_of(i * 384, 128), 384)
        left = mm_tn(whole[:, lanes], g_all[...]).astype(bf16).reshape(2, 2, 96, COLS)
        right = mm_tn(back[:, lanes], gated[...]).astype(bf16).reshape(2, 2, 96, IN)
        for k in range(2):
            grads[2 * i + k, :, :, :COLS] = left[k]
            grads[2 * i + k, :, :, COLS:] = right[k]
        return carry

    lax.fori_loop(0, 4, product, 0)
    swap = send(grads.at[:, 1 - place.core], core_in, place.mate)
    next(plan)
    swap.wait_recv()

    def fold(i, carry):
        total = grads[i, place.core].astype(f32) + core_in[i].astype(f32)
        grads[i, place.core] = total.astype(bf16)
        return carry

    lax.fori_loop(0, 8, fold, 0)
    hops = []
    for k in range(3):
        z = (place.z + k + 1) % 4
        for y in range(2):
            hops.append(send(grads.at[4 * y + z, place.core], z_in.at[k, y], place.along[k]))
    next(plan)
    next(plan)
    for hop in hops:
        hop.wait_recv()

    def joined(y):
        total = grads[4 * y + place.z, place.core].astype(f32)
        for k in range(3):
            total = total + z_in[k, y].astype(f32)
        return total

    y_out[...] = joined(1 - place.ylo).astype(bf16)
    cross = send(y_out, w_in, place.beside)
    next(plan)
    cross.wait_recv()
    mine = joined(place.ylo) + w_in[...].astype(f32)
    mine_grad[...] = mine
    side_box[place.mp] = mine[:, 2 * IN : COLS].astype(bf16)
    sides = [send(side_box.at[place.mp], side_box.at[place.mp], peer) for peer in place.group]
    for copy in early:
        copy.wait_recv()
    copied = sums_box[0]
    for k in range(1, DP):
        copied = copied + sums_box[k]
    copy_sums[...] = copied
    inbox[place.mp] = copied[:8, IN:]
    shares = [send(inbox.at[place.mp], inbox.at[place.mp], peer) for peer in place.group]
    finish(plan)

    gain_row = norm_gain[...]
    gain_sum = jnp.zeros((1, D), f32)
    for i in range(BLOCKS):
        x = tokens[i].astype(f32)
        s = scale[i]
        g = summed[i]
        dot = jnp.sum(g * gain_row * x, axis=1, keepdims=True)
        token_grad[i] = grad_out[i].astype(f32) + s * gain_row * g - x * (s * s * s * dot * (1.0 / D))
        gain_sum = gain_sum + jnp.sum(g * x * s, axis=0, keepdims=True)
    gain_box[place.mp] = jnp.concatenate([gain_sum, jnp.zeros((7, D), f32)], 0)
    gains = [send(gain_box.at[place.mp], gain_box.at[place.mp], peer) for peer in place.group]

    for copy in sides + shares:
        copy.wait_recv()
    both, steps = 0.0, 0.0
    lane = lax.broadcasted_iota(jnp.int32, (N, N), 1)
    source = lax.broadcasted_iota(jnp.int32, (N, N), 0)
    shared = inbox[0]
    for k in range(GROUP):
        piece = side_box[k]
        both = both + piece[:, : 2 * N].astype(f32)
        spot = jnp.where((lane == source + HD * k) & (source < HD), 1.0, 0.0).astype(bf16)
        steps = steps + mm(piece[:, 2 * N :], spot)
        if k:
            shared = shared + inbox[k]
    side_grad[...] = jnp.concatenate([both, steps], 1)
    shared_sums[...] = shared
    for copy in gains:
        copy.wait_recv()
    total = gain_box[0]
    for k in range(1, GROUP):
        total = total + gain_box[k]
    gain_all[place.dp] = total
    ends = [send(gain_all.at[place.dp], gain_all.at[place.dp], peer) for peer in place.copies]
    for copy in ends:
        copy.wait_recv()
    total = gain_all[0]
    for k in range(1, DP):
        total = total + gain_all[k]
    gain_grad[...] = total
    send.drain()


def call(kernel, outs, scratch, sems, collective, args, flops, anywhere=False):
    space = pl.ANY if anywhere else pltpu.VMEM
    return pl.pallas_call(
        kernel,
        out_shape=[jax.ShapeDtypeStruct(shape, dtype) for shape, dtype in outs],
        in_specs=[pl.BlockSpec(memory_space=space)] * len(args),
        out_specs=[pl.BlockSpec(memory_space=space)] * len(outs),
        scratch_shapes=list(scratch)
        + [pltpu.SemaphoreType.DMA((sems,)), pltpu.SemaphoreType.DMA((sems,))]
        + ([pltpu.SemaphoreType.DMA((3,))] if anywhere else []),
        compiler_params=pltpu.CompilerParams(
            collective_id=collective, has_side_effects=True, vmem_limit_bytes=VMEM_BYTES
        ),
        cost_estimate=pl.CostEstimate(
            flops=flops,
            bytes_accessed=sum(a.size * a.dtype.itemsize for a in args),
            transcendentals=0,
        ),
        name=kernel.__name__,
    )(*args)


def on_device(
    tokens,
    seq_len,
    norm_gain,
    main_weight,
    side_weight,
    side_terms,
    channel_terms,
    head_terms,
    output_weight,
    cotangent,
):
    place = lax.axis_index("mp")
    count = BLOCKS * L
    seq = tokens[0].astype(f32)
    scale = lax.rsqrt(jnp.mean(seq * seq, axis=-1, keepdims=True) + epsilon)
    normed = (seq * scale * norm_gain).astype(bf16)
    grad_out = cotangent[0].astype(f32)
    positions = (
        jnp.arange(BLOCKS)[:, None] * L + place * PIECE + jnp.arange(PIECE)[None, :]
    )
    valid = (positions < seq_len[0]).astype(f32)[:, :, None]
    grad_branch = (valid * grad_out).astype(bf16)
    own_steps = lax.dynamic_slice_in_dim(side_weight, 2 * N + place * HD, HD, 1)
    own_weights = jnp.concatenate(
        [
            main_weight.reshape(-1, 2 * IN),
            side_weight[:, : 2 * N],
            own_steps,
            jnp.zeros((own_steps.shape[0], N - HD), bf16),
            output_weight.T,
        ],
        1,
    )
    taps = jnp.concatenate([channel_terms[: CONV + 1], side_terms], 1)
    taps = jnp.concatenate([taps, jnp.zeros((3, MIX), f32)], 0)
    gain = channel_terms[CONV + 1 :]
    heads = jnp.zeros((8, N), f32)
    heads = heads.at[0, :HD].set(head_terms[0]).at[1, :HD].set(-jnp.exp(head_terms[1]))
    skip = jnp.repeat(head_terms[2], PW)[None]

    whole, weights, back = call(
        gather_kernel,
        [
            ((BLOCKS, GROUP, PIECE, D), bf16),
            ((DP, D // DP, COLS + IN), bf16),
            ((BLOCKS, GROUP, PIECE, D), bf16),
        ],
        [], 80, 0, [normed, own_weights, grad_branch], 0, True,
    )
    whole, back = whole.reshape(count, D), back.reshape(count, D)
    weights = weights.reshape(D, COLS + IN)
    raw, gates, steps, scan, mixed, states, g_gated, sums = call(
        forward_kernel,
        [
            ((count + 8, MIX), f32),
            ((count, IN), f32),
            ((count, N), f32),
            ((count, IN), f32),
            ((count, IN), f32),
            ((BLOCKS + 1, N, IN), f32),
            ((count, IN), f32),
            ((L, 128), f32),
        ],
        [pltpu.VMEM((L, 128), f32), pltpu.VMEM((N, IN), f32), pltpu.VMEM((GROUP, 16, L), f32)],
        7, 1, [whole, weights, back, taps, heads, skip, gain], 12 * 10**9,
    )
    g_all, gated, branch, totals = call(
        backward_kernel,
        [
            ((count, COLS), bf16),
            ((count, IN), bf16),
            ((BLOCKS, PIECE, D), f32),
            ((16, MIX), f32),
        ],
        [pltpu.VMEM((BLOCKS, GROUP, PIECE, D), bf16)]
        + SCATTER_SCRATCH
        + [pltpu.VMEM((N, IN), f32), pltpu.VMEM((8, MIX), f32)],
        32, 2,
        [raw, gates, steps, scan, mixed, states, g_gated, sums, weights, taps, heads, skip, gain],
        8 * 10**9,
    )
    result = (seq + valid * branch).astype(bf16)
    token_grad, gain_grad, mine_grad, side_grad, shared_sums, copy_sums = call(
        last_kernel,
        [
            ((BLOCKS, PIECE, D), f32),
            ((8, D), f32),
            ((D // DP, COLS + IN), f32),
            ((D // DP, 3 * N), f32),
            ((8, 2 * N), f32),
            ((16, MIX), f32),
        ],
        [pltpu.VMEM((BLOCKS, GROUP, PIECE, D), bf16)]
        + SCATTER_SCRATCH
        + [
            pltpu.VMEM((BLOCKS, PIECE, D), f32),
            pltpu.VMEM((8, 2, D // DP, COLS + IN), bf16),
            pltpu.VMEM((8, D // DP, COLS + IN), bf16),
            pltpu.VMEM((3, 2, D // DP, COLS + IN), bf16),
            pltpu.VMEM((D // DP, COLS + IN), bf16),
            pltpu.VMEM((D // DP, COLS + IN), bf16),
            pltpu.VMEM((GROUP, 8, 2 * N), f32),
            pltpu.VMEM((GROUP, D // DP, 3 * N), bf16),
            pltpu.VMEM((DP, 16, MIX), f32),
            pltpu.VMEM((GROUP, 8, D), f32),
            pltpu.VMEM((DP, 8, D), f32),
        ],
        96, 3,
        [whole, back, gated, g_all, weights, tokens[0], scale, cotangent[0], norm_gain[None], totals],
        15 * 10**9,
    )
    main_grad = mine_grad[:, : 2 * IN].reshape(-1, 2, IN)
    out_grad = mine_grad[:, COLS:].T
    conv_total = shared_sums[: CONV + 1]
    channel_total = copy_sums[: CONV + 2, :IN]
    decay = heads[1, :HD] * copy_sums[CONV + 3, :HD]
    skip_total = copy_sums[CONV + 2, :IN].reshape(HD, PW).sum(1)
    head_total = jnp.stack([copy_sums[CONV + 3, N : N + HD], decay, skip_total])
    return (
        result[None],
        token_grad[None],
        gain_grad[0],
        main_grad,
        side_grad[:, : 2 * N + 48],
        conv_total,
        channel_total,
        head_total,
        out_grad,
    )


def solution(mesh):
    placed = (
        P("dp", None, "mp", None),
        P("dp"),
        P(),
        P("dp", None, "mp"),
        P("dp", None),
        P(),
        P(None, "mp"),
        P(None, "mp"),
        P("mp", "dp"),
        P("dp", None, "mp", None),
    )
    return jax.shard_map(
        on_device,
        mesh=mesh,
        in_specs=placed,
        out_specs=(
            P("dp", None, "mp", None),
            P("dp", None, "mp", None),
            P(),
            P("dp", None, "mp"),
            P("dp", None),
            P(),
            P(None, "mp"),
            P(None, "mp"),
            P("mp", "dp"),
        ),
        check_vma=False,
    )
```

time: 1440 us -> 419 us (0.29)
  waiting for transfers between devices: 456 us -> 0 us
  Pallas kernels: 0 us -> 395 us
  local copies, waits for them, and re-layouts: 340 us -> 17.3 us
  blocking collectives: 215 us -> 0 us
  other arithmetic: 206 us -> 4.91 us
  matrix products: 194 us -> 0 us
    pallas_call x0 -> x4, Pallas kernels: none -> 395 us  [call(): pl.pallas_call(kernel, out_shape=[jax.ShapeDtypeStruct(shape, dtype) for...]
    reduce_scatter x6 -> x0, waiting for transfers between devices: 363 us -> none  [the longest x1 121 us: on_device(): lax.psum_scatter(norm_part.reshape(stretches, span, width), 'mp', scatter...]
    dot_general x121 -> x0, matrix products: 194 us -> none  [the longest x24 56.5 us: block_step(): inner = jnp.einsum('tsh,shp->thp', mixing, values, precision=highest)]
    psum x5 -> x0, blocking collectives: 187 us -> none  [the longest x1 65 us: on_device(): lax.psum((norm_part_gain, grad_side_terms), ('dp', 'mp'))]
    dynamic_update_slice x32 -> x0, local copies, waits for them, and re-layouts: 170 us -> none  [state_scan(): final, outputs = lax.scan(jax.checkpoint(partial_step(decay)), start, parts)]
    another operation x81 -> x1, other arithmetic: 120 us -> 0.59 us  [on_device(): head_total = jnp.stack([copy_sums[CONV + 3, N:N + HD], decay, skip_total])]
    all_gather x4 -> x0, waiting for transfers between devices: 91.9 us -> none  [the longest x1 88.3 us: on_device(): lax.all_gather(normed, 'mp', axis=1, tiled=True).reshape(count, width)]
    another operation x116 -> x2, local copies, waits for them, and re-layouts: 50.8 us -> 0.72 us  [the longest x1 0.64 us: on_device(): skip = jnp.repeat(head_terms[2], PW)[None]]
  transfers between devices with their start and end apart: 10 -> 0, of which waited for: 7 -> 0; matrix products, arithmetic and copies ran while one was open for 27% -> 0% of each run, Pallas kernels for 0% -> 0%
where the time goes in v1:
time: 419 us
  Pallas kernels  395 us (94%)
  local copies, waits for them, and re-layouts  17.3 us (4%)
  other arithmetic  4.91 us (1%)
    pallas_call x4, Pallas kernels, call(): pl.pallas_call(kernel, out_shape=[jax.ShapeDtypeStruct(shape, dtype) for...  395 us

profile of v1, /device:TPU:1, one launch (start us, length us, event | category | flops | bytes accessed | tf_op | source)
XLA Modules:
  0.0 419.0 jit_solution(1146779176307779544)
XLA Ops:
  0.6 0.0 copy-start
  0.7 0.0 copy-start.6
  0.7 0.0 copy-start.4
  0.7 0.9 constant_dynamic-slice_fusion
  1.6 0.9 copy.20
  2.5 0.8 slice.81
  3.4 1.7 concatenate.13.weights
  5.7 0.1 fusion.5
  5.8 0.0 copy-done
  5.8 0.2 fusion
  6.0 0.0 copy-done.6
  6.0 0.0 copy-done.4
  6.0 1.4 fusion.2
  7.5 0.0 copy-start.11
  7.5 0.0 copy-start.7
  7.5 0.0 copy-start.8
  7.5 159.2 %gather_kernel.1 = (bf16[8,8,32,1536]{3,2,1,0:T(8,128)(2,1)}, bf16[16,96,1536]{2,1,0:T(8,128)(2,1)}, bf16[8,8,32,1536]{3,2,1,0:T(8,128)(2,1)}) custom-call(bf16[8,32,1536]{2,1,0:T(8,128)(2,1)} %get-tuple-element.82.normed, bf16[96,1536]{1,0:T(8,128)(2,1)} %concatenate.13.weights, bf16[8,32,1536]{2,1,0:T(8,128)(2,1)} %get-tuple-element.83.grad), custom_call_target="tpu_custom_call" | custom-call | bytes 1867776 | tf_op jit(solution)/shard_map/gather_kernel/pallas_call | solution.py:690
  166.7 0.0 copy-done.11
  166.8 0.2 scatter.9.heads
  167.0 0.0 copy-start.10
  167.0 0.1 broadcast_in_dim.11
  167.1 0.6 broadcast_in_dim_reshape.3.skip
  167.7 0.0 copy-done.7
  167.7 0.0 copy-done.8
  167.7 0.6 select_maximum_fusion.taps
  168.3 0.6 slice.86.gain
  168.9 0.0 copy-done.10
  168.9 46.3 %forward_kernel.1 = (f32[2056,640]{1,0:T(8,128)}, f32[2048,384]{1,0:T(8,128)}, f32[2048,128]{1,0:T(8,128)}, f32[2048,384]{1,0:T(8,128)}, f32[2048,384]{1,0:T(8,1...) custom-call(bf16[2048,1536]{1,0:T(8,128)(2,1)} %bitcast.37, bf16[1536,1536]{1,0:T(8,128)(2,1)} %bitcast.41, ...), custom_call_target="tpu_custom_call" | custom-call | flops 12000000000 | bytes 17329152 | tf_op jit(solution)/shard_map/forward_kernel/pallas_call | solution.py:690
  215.2 83.2 %backward_kernel.1 = (bf16[2048,1152]{1,0:T(8,128)(2,1)}, bf16[2048,384]{1,0:T(8,128)(2,1)}, f32[8,32,1536]{2,1,0:T(8,128)}, f32[16,640]{1,0:T(8,128)}) custom-call(f32[2056,640]{1,0:T(8,128)} %get-tuple-element.57.raw, f32[2048,384]{1,0:T(8,128)} %get-tuple-element.58.gates, f32[2048,128]{1,0:T(8,128)} %get-tuple-element.59.steps, ...), custom_call_target="tpu_custom_call" | custom-call | flops 8000000000 | bytes 25541632 | tf_op jit(solution)/shard_map/backward_kernel/pallas_call | solution.py:690
  298.4 0.8 copy.19.scale
  299.2 0.6 broadcast_in_dim.25.norm_gain
  299.8 0.0 copy-start.2
  299.8 106.6 %last_kernel.1 = (f32[8,32,1536]{2,1,0:T(8,128)}, f32[8,1536]{1,0:T(8,128)}, f32[96,1536]{1,0:T(8,128)}, f32[96,384]{1,0:T(8,128)}, f32[8,256]{1,0:T(8,128)}, /*index=5*/f32[16,640]{1,0:T(8,128)}) custom-call(bf16[2048,1536]{1,0:T(8,128)(2,1)} %bitcast.38, bf16[2048,1536]{1,0:T(8,128)(2,1)} %bitcast.40, bf16[2048,384]{1,0:T(8,128)(2,1)} %get-tuple-element.66.gated, ...), custom_call_target="tpu_custom_call" | custom-call | flops 15000000512 | bytes 25213952 | tf_op jit(solution)/shard_map/last_kernel/pallas_call | solution.py:690
  406.4 0.0 copy-start.1
  406.4 0.8 slice_reduce_fusion.1
  407.2 0.1 reshape_squeeze.3
  407.3 0.1 reduce_sum.19
  407.4 0.7 fusion.7
  408.1 0.6 pad_maximum_fusion
  408.7 1.0 slice.88
  409.7 0.9 reshape.144
  410.5 1.6 slice_bitcast_fusion
  412.1 1.3 slice.91
  413.4 1.4 slice_reduce_fusion
  414.8 0.0 copy-done.2
  414.9 0.0 copy-done.1
  414.9 0.0 copy-start.3
  414.9 1.1 fusion.4
  416.0 0.6 copy-done.3
  416.5 0.0 copy-start.5
  416.5 0.0 copy-start.9
  416.6 1.1 copy.26
  417.7 0.0 copy-done.5
  417.7 0.7 copy.27
  418.4 0.0 copy-done.9
  418.4 0.6 copy.28
  (5 shorter events, 0.0 us)
Async XLA Ops:
  0.6 5.1 %copy-start = (bf16[1,8,32,1536]{3,2,1,0:T(8,128)(2,1)S(1)}, bf16[1,8,32,1536]{3,2,1,0:T(8,128)(2,1)}, u32[]{:S(2)}) copy-start(bf16[1,8,32,1536]{3,2,1,0:T(8,128)(2,1)} %param.14) | copy-start | bytes 2359300
  0.7 5.4 %copy-start.6 = (f32[1536]{0:T(1024)S(1)}, f32[1536]{0:T(1024)}, u32[]{:S(2)}) copy-start(f32[1536]{0:T(1024)} %param.16) | copy-start | bytes 18436
  0.7 5.4 %copy-start.4 = (bf16[1,8,32,1536]{3,2,1,0:T(8,128)(2,1)S(1)}, bf16[1,8,32,1536]{3,2,1,0:T(8,128)(2,1)}, u32[]{:S(2)}) copy-start(bf16[1,8,32,1536]{3,2,1,0:T(8,128)(2,1)} %param.23) | copy-start | bytes 2359300
  7.5 159.2 %copy-start.11 = (f32[3,6]{1,0:T(4,128)S(1)}, f32[3,6]{1,0:T(4,128)}, u32[]{:S(2)}) copy-start(f32[3,6]{1,0:T(4,128)} %param.21) | copy-start | bytes 220
  7.5 160.2 %copy-start.7 = (f32[6,384]{1,0:T(8,128)S(1)}, f32[6,384]{1,0:T(8,128)}, u32[]{:S(2)}) copy-start(f32[6,384]{1,0:T(8,128)} %param.20) | copy-start | bytes 27652
  7.5 160.2 %copy-start.8 = (f32[5,256]{1,0:T(8,128)S(1)}, f32[5,256]{1,0:T(8,128)}, u32[]{:S(2)}) copy-start(f32[5,256]{1,0:T(8,128)} %param.19) | copy-start | bytes 15364
  167.0 1.9 copy-start.10
  299.8 115.1 %copy-start.2 = (f32[8,32,1536]{2,1,0:T(8,128)S(1)}, f32[8,32,1536]{2,1,0:T(8,128)}, u32[]{:S(2)}) copy-start(f32[8,32,1536]{2,1,0:T(8,128)} %get-tuple-element.65) | copy-start | bytes 4718596
  406.4 8.5 %copy-start.1 = (bf16[1,8,32,1536]{3,2,1,0:T(8,128)(2,1)S(1)}, bf16[1,8,32,1536]{3,2,1,0:T(8,128)(2,1)}, u32[]{:S(2)}) copy-start(bf16[1,8,32,1536]{3,2,1,0:T(8,128)(2,1)} %param.14) | copy-start | bytes 2359300
  414.9 1.7 copy-start.3
  416.5 1.1 copy-start.5
  416.5 1.8 copy-start.9

commit v2 on v1

v2 whole, which is shorter than its diff:
```python
import functools

import jax
import jax.numpy as jnp
from jax import lax
from jax.experimental import pallas as pl
from jax.experimental.pallas import tpu as pltpu
from jax.sharding import PartitionSpec as P

f32, bf16 = jnp.float32, jnp.bfloat16
CONV, D, INNER = 4, 1536, 3072
L, N, PW, IN, HD = 256, 128, 64, 384, 6
BLOCKS, GROUP, PIECE, DP = 8, 8, 32, 16
COLS = 2 * IN + 3 * N
MIX = IN + 2 * N
MESH = pl.DeviceIdType.MESH
VMEM_BYTES = 62 * 2**20
epsilon = 1e-05
NEG = -1e30

def mm(a, b):
    return lax.dot_general(a, b, (((1,), (0,)), ((), ())), preferred_element_type=f32)
def mm_nt(a, b):
    return lax.dot_general(a, b, (((1,), (1,)), ((), ())), preferred_element_type=f32)
def mm_tn(a, b):
    return lax.dot_general(a, b, (((0,), (0,)), ((), ())), preferred_element_type=f32)

def thirds(x):
    hi = x.astype(bf16)
    rest = x - hi.astype(f32)
    mid = rest.astype(bf16)
    return hi, mid, (rest - mid.astype(f32)).astype(bf16)

def exact_left(mask, x):
    a, b, c = thirds(x)
    return mm(mask, a) + mm(mask, b) + mm(mask, c)

def exact_right(x, mask):
    a, b, c = thirds(x)
    return mm(a, mask) + mm(b, mask) + mm(c, mask)

def sigmoid(x):
    return 1.0 / (1.0 + jnp.exp(-x))

def softplus(x):
    return jnp.maximum(x, 0.0) + jnp.log1p(jnp.exp(-jnp.abs(x)))

def tri(lower):
    r = lax.broadcasted_iota(jnp.int32, (L, L), 0)
    c = lax.broadcasted_iota(jnp.int32, (L, L), 1)
    return jnp.where((r >= c) if lower else (r <= c), 1.0, 0.0).astype(bf16)

def spread(cols, low):
    out = []
    for j in range(3):
        a = jnp.broadcast_to(cols[:, 2 * j : 2 * j + 1], (cols.shape[0], 128))
        b = jnp.broadcast_to(cols[:, 2 * j + 1 : 2 * j + 2], (cols.shape[0], 128))
        out.append(jnp.where(low, a, b))
    return jnp.concatenate(out, 1)

def conv_pre(window, taps):
    total = taps[4:5]
    for k in range(4):
        total = total + taps[k : k + 1] * window[5 + k : 5 + k + L]
    return total

def low_lanes(rows):
    return lax.broadcasted_iota(jnp.int32, (rows, 128), 1) < 64

def head_quantities(dt_raw, heads):
    pre = dt_raw + heads[0:1]
    dt = softplus(pre)
    logs = exact_left(tri(True), dt * heads[1:2])
    return pre, dt, logs

def half_mask(t):
    rows = 128
    r = lax.broadcasted_iota(jnp.int32, (rows, 128 * (t + 1)), 0) + 128 * t
    c = lax.broadcasted_iota(jnp.int32, (rows, 128 * (t + 1)), 1)
    return r >= c

def weights_of(logs, logs_t, h, t):
    w = 128 * (t + 1)
    col = jnp.broadcast_to(logs[128 * t : 128 * (t + 1), h : h + 1], (128, 128))
    if t:
        col = jnp.concatenate([col, col], 1)
    gap = col - logs_t[h : h + 1, :w]
    return jnp.exp(jnp.where(half_mask(t), gap, NEG))

def fwd_block(window, gates, dt_raw, taps, heads, skip, state):
    low = low_lanes(L)
    total = conv_pre(window, taps)
    act = total * sigmoid(total)
    x, b, c = act[:, :IN], act[:, IN : IN + N].astype(bf16), act[:, IN + N :].astype(bf16)
    pre, dt, logs = head_quantities(dt_raw, heads)
    logs_t = logs.T
    dt_l, logs_l = spread(dt, low), spread(logs, low)
    xd = (dt_l * x).astype(bf16)
    g = mm_nt(c, b)
    half_low = low_lanes(128)
    rows = [[], []]
    zero = jnp.zeros((), bf16)
    for j in range(3):
        pair = xd[:, 128 * j : 128 * (j + 1)]
        own = (jnp.where(low, pair, zero), jnp.where(low, zero, pair))
        for t in range(2):
            w = 128 * (t + 1)
            total_y = 0.0
            for e in range(2):
                m = weights_of(logs, logs_t, 2 * j + e, t) * g[128 * t : 128 * (t + 1), :w]
                total_y = total_y + mm(m.astype(bf16), own[e][:w])
            rows[t].append(total_y)
    intra = jnp.concatenate([jnp.concatenate(r, 1) for r in rows], 0)
    scan = intra + jnp.exp(logs_l) * mm(c, state.astype(bf16))
    last = logs_l[L - 1 : L]
    tails = jnp.exp(last - logs_l)
    state = jnp.exp(last) * state + mm_tn(b, (tails * xd.astype(f32)).astype(bf16))
    mixed = (scan + skip * x) * (gates * sigmoid(gates))
    return scan, mixed, state

def bwd_block(window, gates, dt_raw, taps, heads, skip, gain, state, scan, rnorm, products, g_gated, d_state, after):
    low = low_lanes(L)
    total = conv_pre(window, taps)
    sig = sigmoid(total)
    act = total * sig
    d_act = sig + act * (1.0 - sig)
    x, b, c = act[:, :IN], act[:, IN : IN + N].astype(bf16), act[:, IN + N :].astype(bf16)
    pre, dt, logs = head_quantities(dt_raw, heads)
    logs_t = logs.T
    dt_l, logs_l = spread(dt, low), spread(logs, low)
    xd = (dt_l * x).astype(bf16)
    xdf = xd.astype(f32)
    gsig = sigmoid(gates)
    gate = gates * gsig
    y = scan + skip * x
    mixed = y * gate
    g_mixed = rnorm * (g_gated * gain) - mixed * (rnorm * rnorm * rnorm * products * (1.0 / 3072.0))
    gain_sum = jnp.sum(g_gated * mixed * rnorm, axis=0, keepdims=True)
    dy = g_mixed * gate
    d_gates = g_mixed * y * (gsig + gate * (1.0 - gsig))
    skip_sum = jnp.sum(dy * x, axis=0, keepdims=True)
    dyb = dy.astype(bf16)
    g = mm_nt(c, b)
    zero = jnp.zeros((), bf16)
    dg = [0.0, 0.0]
    parts = []
    for j in range(3):
        pair_x = xd[:, 128 * j : 128 * (j + 1)]
        pair_y = dyb[:, 128 * j : 128 * (j + 1)]
        own = (jnp.where(low, pair_y, zero), jnp.where(low, zero, pair_y))
        upper, lower = 0.0, 0.0
        for e in range(2):
            for t in range(2):
                w = 128 * (t + 1)
                wt = weights_of(logs, logs_t, 2 * j + e, t)
                mine = own[e][128 * t : 128 * (t + 1)]
                dm = mm_nt(mine, pair_x[:w])
                dg[t] = dg[t] + dm * wt
                m = (wt * g[128 * t : 128 * (t + 1), :w]).astype(bf16)
                back = mm_tn(m, mine)
                upper = upper + back[:128]
                if t:
                    lower = lower + back[128:]
        parts.append(jnp.concatenate([upper, lower], 0))
    d_intra = jnp.concatenate(parts, 1)
    e_l = jnp.exp(logs_l)
    last = logs_l[L - 1 : L]
    tails = jnp.exp(last - logs_l)
    sb = state.astype(bf16)
    dsb = d_state.astype(bf16)
    edy = (e_l * dy).astype(bf16)
    txd = (tails * xdf).astype(bf16)
    v = mm(b, dsb)
    dxd = d_intra + tails * v
    dg0, dg1 = dg[0].astype(bf16), dg[1].astype(bf16)
    dc = mm_nt(edy, sb) + jnp.concatenate([mm(dg0, b[:128]), mm(dg1, b)], 0)
    first = mm_tn(dg0, c[:128])
    second = mm_tn(dg1, c[128:])
    db = mm_nt(txd, dsb) + jnp.concatenate([first + second[:128], second[128:]], 0)
    z = dyb.astype(f32) * scan - xdf * d_intra - txd.astype(f32) * v
    kept = jnp.sum(state * dsb.astype(f32), axis=0, keepdims=True)
    boundary = jnp.exp(last) * kept + jnp.sum(txd.astype(f32) * v, axis=0, keepdims=True)
    row = lax.broadcasted_iota(jnp.int32, (L, IN), 0)
    z = jnp.where(row == L - 1, z + boundary, z)
    r = lax.broadcasted_iota(jnp.int32, (IN, 128), 0)
    cc = lax.broadcasted_iota(jnp.int32, (IN, 128), 1)
    fold = jnp.where((r // PW) == cc, 1.0, 0.0).astype(bf16)
    dl = exact_right(z, fold)
    g_adt = exact_left(tri(False), dl)
    direct = exact_right(x * dxd, fold)
    d_pre = (direct + heads[1:2] * g_adt) * sigmoid(pre)
    decay_sum = jnp.sum(dt * g_adt, axis=0, keepdims=True)
    bias_sum = jnp.sum(d_pre, axis=0, keepdims=True)
    d_state = jnp.exp(last) * d_state + mm_tn(c, edy)
    dx = dt_l * dxd + skip * dy
    g_pre = jnp.concatenate([dx, db, dc], 1) * d_act
    longer = jnp.concatenate([g_pre, after], 0)
    d_raw = 0.0
    tap_sums = []
    for k in range(4):
        d_raw = d_raw + taps[k : k + 1] * longer[3 - k : 3 - k + L]
        tap_sums.append(jnp.sum(g_pre * window[5 + k : 5 + k + L], axis=0, keepdims=True))
    tap_sums.append(jnp.sum(g_pre, axis=0, keepdims=True))
    g_all = jnp.concatenate([d_gates.astype(bf16), d_raw.astype(bf16), d_pre.astype(bf16)], 1)
    return g_all, d_state, g_pre[:8], (jnp.concatenate(tap_sums, 0), gain_sum, skip_sum, decay_sum, bias_sum)


class Place:
    def __init__(self):
        dp, mp = lax.axis_index("dp"), lax.axis_index("mp")
        self.dp, self.mp = dp, mp
        self.hi, self.x = mp // 4, mp % 4
        self.lo = 1 - self.hi
        self.ylo, self.z, self.core = dp // 8, (dp // 2) % 4, dp % 2
        self.other_core = 1 - self.core
        self.mine, self.theirs = self.hi * 4, self.lo * 4
        self.xs = [(self.x + k) % 4 for k in range(4)]
        self.row = [self.mine + x for x in self.xs]
        self.far_row = [self.theirs + x for x in self.xs]
        self.right, self.left = (dp, self.row[1]), (dp, self.row[3])
        self.across = (dp, self.far_row[0])
        self.mate = (dp + 1 - 2 * self.core, mp)
        self.beside_dp = self.at(1 - self.ylo, self.z)
        self.beside = (self.beside_dp, mp)
        self.zs = [(self.z + k) % 4 for k in range(4)]
        self.near_dp = [self.at(self.ylo, z) for z in self.zs]
        self.far_dp = [self.at(1 - self.ylo, z) for z in self.zs]
        self.near_slot = [self.ylo * 4 + z for z in self.zs]
        self.far_slot = [(1 - self.ylo) * 4 + z for z in self.zs]
        self.along = [(self.near_dp[k], mp) for k in (1, 2, 3)]
        self.group = [(dp, (mp + k) % GROUP) for k in range(1, GROUP)]
        self.copies = [((dp + k) % DP, mp) for k in range(1, DP)]

    def at(self, ylo, z):
        return ylo * 8 + z * 2 + self.core


def meet(peers):
    barrier = pltpu.get_barrier_semaphore()
    for peer in peers:
        pl.semaphore_signal(barrier, inc=1, device_id=peer, device_id_type=MESH)
    pl.semaphore_wait(barrier, len(peers))


class View:
    def __init__(self, ref, *chain):
        self.ref, self.chain = ref, chain

    @property
    def at(self):
        return Indexer(self)

    def build(self):
        ref = self.ref
        for index in self.chain:
            ref = ref.at[index]
        return ref

    def __getitem__(self, index):
        return self.build()[index]

    def __setitem__(self, index, value):
        self.build()[index] = value


class Indexer:
    def __init__(self, view):
        self.view = view

    def __getitem__(self, index):
        return View(self.view.ref, *self.view.chain, index)


class Copy:
    def __init__(self, make):
        self.make = make
        make().start()

    def wait(self):
        self.make().wait()

    def wait_recv(self):
        self.make().wait_recv()

    def wait_send(self):
        self.make().wait_send()


class Sender:
    def __init__(self, send_sem, recv_sem, local_sem):
        self.send_sem, self.recv_sem, self.local_sem = send_sem, recv_sem, local_sem
        self.count, self.started, self.locals = 0, [], 0

    def __call__(self, source, target, peer):
        k = self.count
        self.count += 1
        copy = Copy(
            lambda: pltpu.make_async_remote_copy(
                src_ref=source.build(),
                dst_ref=target.build(),
                send_sem=self.send_sem.at[k],
                recv_sem=self.recv_sem.at[k],
                device_id=peer,
                device_id_type=MESH,
            )
        )
        self.started.append(copy)
        return copy

    def local(self, source, target):
        k = self.locals
        self.locals += 1
        return Copy(
            lambda: pltpu.make_async_copy(source.build(), target.build(), self.local_sem.at[k])
        )

    def drain(self):
        for copy in self.started:
            copy.wait_send()
        self.started = []


def step(plan, count=1):
    for _ in range(count):
        next(plan, None)


def finish(plan):
    for _ in plan:
        pass


def gather_unit(send, place, buf, first, second):
    me, lx, rx, ox = place.row[0], place.row[3], place.row[1], place.row[2]
    ym, lxy, rxy = place.far_row[0], place.far_row[3], place.far_row[1]
    right, left, across = place.right, place.left, place.across
    half = PIECE // 2

    def go(block, slot, h, to):
        part = buf.at[block, slot, pl.ds(half * h, half)]
        return send(part, part, to)

    c = [go(second, me, 0, across), go(second, me, 1, across)]
    a = [go(first, me, 0, right), go(first, me, 1, left)]
    a += [go(first, me, 1, right), go(first, me, 0, left)]
    b = [go(second, me, 0, right), go(second, me, 1, left)]
    b += [go(second, me, 1, right), go(second, me, 0, left)]
    y = [go(first, me, 0, across), go(first, me, 1, across)]
    yield
    a[0].wait_recv()
    f = [go(first, lx, 0, right)]
    y.append(go(first, lx, 0, across))
    a[1].wait_recv()
    f.append(go(first, rx, 1, left))
    y.append(go(first, rx, 1, across))
    yield
    a[2].wait_recv()
    y.append(go(first, lx, 1, across))
    a[3].wait_recv()
    y.append(go(first, rx, 0, across))
    yield
    b[0].wait_recv()
    k = [go(second, lx, 0, right)]
    b[1].wait_recv()
    k.append(go(second, rx, 1, left))
    c[0].wait_recv()
    c[1].wait_recv()
    d = [go(second, ym, 0, right), go(second, ym, 1, left)]
    d += [go(second, ym, 1, right), go(second, ym, 0, left)]
    yield
    f[0].wait_recv()
    y.append(go(first, ox, 0, across))
    f[1].wait_recv()
    y.append(go(first, ox, 1, across))
    yield
    d[0].wait_recv()
    e = [go(second, lxy, 0, right)]
    d[1].wait_recv()
    e.append(go(second, rxy, 1, left))
    yield
    for copy in [b[2], b[3], d[2], d[3]] + k + e + y:
        copy.wait_recv()
    yield


def row_gather_unit(send, place, buf, first):
    me, lx, rx = place.xs[0], place.xs[3], place.xs[1]

    def go(block, slot, to):
        part = buf.at[block, slot]
        return send(part, part, to)

    a = [go(first, me, place.right), go(first + 1, me, place.left)]
    a += [go(first + 1, me, place.right), go(first, me, place.left)]
    yield
    a[0].wait_recv()
    f = [go(first, lx, place.right)]
    a[1].wait_recv()
    f.append(go(first + 1, rx, place.left))
    yield
    for copy in a[2:] + f:
        copy.wait_recv()
    yield


def weight_steps(send, place, buf):
    def go(slot, peer):
        return send(buf.at[slot], buf.at[slot], peer)

    own, other = place.dp, place.beside_dp
    one = go(own, place.beside)
    near = [go(own, peer) for peer in place.along]
    mates = [go(own, place.mate)]
    yield
    one.wait_recv()
    far = [go(other, peer) for peer in place.along]
    mates.append(go(other, place.mate))
    yield
    for k in range(3):
        near[k].wait_recv()
        mates.append(go(place.near_dp[3 - k], place.mate))
    yield
    for k in range(3):
        far[k].wait_recv()
        mates.append(go(place.far_dp[3 - k], place.mate))
    yield
    for copy in mates:
        copy.wait_recv()
    yield


def add_into(target, other):
    target[...] = (target[...].astype(f32) + other[...].astype(f32)).astype(bf16)


def scatter_unit(send, place, buf, first, second, y_in, x_in, xx_in, t_out, t_in, total):
    right, left, across = place.right, place.left, place.across
    half = PIECE // 2
    mine, theirs = place.row, place.far_row
    order = (2, 1, 3, 0)

    def first_hop(k, block, side):
        slot = side[2]
        return [
            send(buf.at[block, slot, pl.ds(0, half)], x_in.at[k, 0], right),
            send(buf.at[block, slot, pl.ds(half, half)], x_in.at[k, 1], left),
        ]

    def second_hop(k, block, side, hops):
        hops[0].wait_recv()
        add_into(buf.at[block, side[1], pl.ds(0, half)], x_in.at[k, 0])
        one = send(buf.at[block, side[1]], xx_in.at[k, 0], right)
        hops[1].wait_recv()
        add_into(buf.at[block, side[3], pl.ds(half, half)], x_in.at[k, 1])
        return [one, send(buf.at[block, side[3]], xx_in.at[k, 1], left)]

    def three(k, block, side):
        return (
            buf[block, side[0]].astype(f32) + xx_in[k, 0].astype(f32) + xx_in[k, 1].astype(f32)
        )

    ahead = [send(buf.at[first, theirs[n]], y_in.at[k], across) for k, n in enumerate(order)]
    hop_t = first_hop(1, second, theirs)
    hop_m = first_hop(2, second, mine)
    yield
    two_t = second_hop(1, second, theirs, hop_t)
    yield
    ahead[0].wait_recv()
    add_into(buf.at[first, mine[2]], y_in.at[0])
    hop_a = first_hop(0, first, mine)
    two_m = second_hop(2, second, mine, hop_m)
    yield
    for copy in two_t:
        copy.wait_recv()
    t_out[...] = three(1, second, theirs).astype(bf16)
    last = send(t_out, t_in, across)
    yield
    for k in range(1, 4):
        ahead[k].wait_recv()
        add_into(buf.at[first, mine[order[k]]], y_in.at[k])
    two_a = second_hop(0, first, mine, hop_a)
    yield
    for copy in two_m + [last]:
        copy.wait_recv()
    total[second] = three(2, second, mine) + t_in[...].astype(f32)
    yield
    for copy in two_a:
        copy.wait_recv()
    total[first] = three(0, first, mine)
    yield


def row_scatter_unit(send, place, buf, first, x_in, xx_in, keep):
    xs = place.xs
    hops = [
        send(buf.at[first, xs[2]], x_in.at[0], place.right),
        send(buf.at[first + 1, xs[2]], x_in.at[1], place.left),
    ]
    yield
    hops[0].wait_recv()
    add_into(buf.at[first, xs[1]], x_in.at[0])
    two = [send(buf.at[pl.ds(first, 2), xs[1]], xx_in.at[0], place.right)]
    hops[1].wait_recv()
    add_into(buf.at[first + 1, xs[3]], x_in.at[1])
    two.append(send(buf.at[pl.ds(first, 2), xs[3]], xx_in.at[1], place.left))
    yield
    for copy in two:
        copy.wait_recv()
    for k in range(2):
        total = buf[first + k, xs[0]].astype(f32)
        keep(first + k, total + xx_in[0, k].astype(f32) + xx_in[1, k].astype(f32))
    yield


def reduce_steps(send, place, grads, swaps, core_in, z_in, y_out, w_in, keep):
    core = place.core
    for i, swap in enumerate(swaps):
        swap.wait_recv()
        for k in (2 * i, 2 * i + 1):
            add_into(grads.at[k, core], core_in.at[k])
    hops = []
    for k in range(3):
        for y, slots in enumerate((place.far_slot, place.near_slot)):
            slot = slots[k + 1]
            hops.append(send(grads.at[slot, core], z_in.at[k, y], place.along[k]))
    yield

    def joined(y, slots):
        total = grads[slots[0], core].astype(f32)
        for k in range(3):
            total = total + z_in[k, y].astype(f32)
        return total

    for hop in hops[::2]:
        hop.wait_recv()
    y_out[...] = joined(0, place.far_slot).astype(bf16)
    cross = send(y_out, w_in, place.beside)
    yield
    for hop in hops[1::2]:
        hop.wait_recv()
    cross.wait_recv()
    keep(joined(1, place.near_slot) + w_in[...].astype(f32))
    yield


def rows(block, count=L):
    return pl.ds(pl.multiple_of(block * count, count), count)


def pick(columns, block):
    lane = lax.broadcasted_iota(jnp.int32, columns.shape, 1)
    return jnp.sum(jnp.where(lane == block, columns, 0.0), axis=1, keepdims=True)


def run_blocks(body, hooks):
    def one(i, carry):
        body(i)
        for k, hook in hooks.items():
            pl.when(i == k)(hook)
        return carry

    lax.fori_loop(0, BLOCKS, one, 0)


def front_kernel(
    normed, own_weights, own_out, grad, taps, heads, skip, gain,
    whole_o, weights_o, out_o, back_o, raw_o, gates_o, steps_o, scan_o, states_o, g_gated_o, gated_o, sums,
    whole, weights, out, back, raw, gates, steps, scan, mixed, states, g_gated, gated, halves,
    squares, state, inbox, send_sem, recv_sem, local_sem,
):
    (
        normed, own_weights, own_out, grad, taps, heads, skip, gain, whole_o, weights_o, out_o,
        back_o, raw_o, gates_o, steps_o, scan_o, states_o, g_gated_o, gated_o, sums, whole,
        weights, out, back, raw, gates, steps, scan, mixed, states, g_gated, gated, halves,
        squares, state, inbox,
    ) = map(
        View,
        (
            normed, own_weights, own_out, grad, taps, heads, skip, gain, whole_o, weights_o, out_o,
            back_o, raw_o, gates_o, steps_o, scan_o, states_o, g_gated_o, gated_o, sums, whole,
            weights, out, back, raw, gates, steps, scan, mixed, states, g_gated, gated, halves,
            squares, state, inbox,
        ),
    )
    place = Place()
    whole[:, place.mp] = normed[...]
    weights[place.dp] = own_weights[...]
    out[place.dp, :, :IN] = own_out[...]
    back[:, place.xs[0]] = grad[...]
    meet(place.group + [place.mate, place.beside] + place.along)
    send = Sender(send_sem, recv_sem, local_sem)
    units = [gather_unit(send, place, whole, 2 * u, 2 * u + 1) for u in range(4)]
    columns = weight_steps(send, place, weights)
    outs = weight_steps(send, place, out)
    backs = [row_gather_unit(send, place, back, 2 * u) for u in range(4)]
    stored = []

    step(columns)
    pair = send(own_out, out.at[place.dp, :, pl.ds(IN, IN)], place.across)
    step(units[0])
    step(columns)
    step(units[1])
    step(units[0], 2)
    step(units[2])
    step(units[0], 2)
    step(columns)
    step(units[1], 2)
    step(units[3])
    step(units[0], 2)
    step(units[1], 2)
    step(columns)
    pair.wait_recv()
    step(outs)
    step(units[2], 2)
    step(units[1], 2)
    step(columns)

    raw[pl.ds(0, 8)] = jnp.zeros((8, MIX), f32)
    state[...] = jnp.zeros((N, IN), f32)
    squares[...] = jnp.zeros((L, 128), f32)
    lane = lax.broadcasted_iota(jnp.int32, (L, 128), 1)

    def body(i):
        at = rows(i)
        both = mm(whole[i].reshape(L, D), weights[...].reshape(D, COLS))
        gates[at] = both[:, :IN]
        steps[at] = both[:, IN + MIX :]
        raw[pl.ds(pl.multiple_of(i * L + 8, 8), L)] = both[:, IN : IN + MIX]
        states[i] = state[...]
        window = raw[pl.ds(pl.multiple_of(i * L, 8), L + 8)]
        inner, outer, after = fwd_block(
            window, gates[at], steps[at], taps[...], heads[...], skip[...], state[...]
        )
        scan[at] = inner
        mixed[at] = outer
        state[...] = after
        square = jnp.sum(outer * outer, axis=1, keepdims=True)
        squares[...] = jnp.where(lane == i, square, squares[...])

    def hook_0():
        step(units[2], 2)
        step(units[3], 2)
        step(outs)

    def hook_1():
        step(units[2], 3)
        step(units[3], 2)
        for unit in backs:
            step(unit)

    def hook_2():
        step(units[3], 1)
        step(outs)

    def hook_3():
        step(units[3], 2)
        step(backs[0])
        step(outs)

    def hook_4():
        step(backs[1])
        step(outs)

    def hook_5():
        step(backs[2])
        stored.append(send.local(whole, whole_o))
        stored.append(send.local(weights, weights_o))

    def hook_6():
        step(backs[3])
        stored.append(send.local(out, out_o))

    run_blocks(
        body,
        {0: hook_0, 1: hook_1, 2: hook_2, 3: hook_3, 4: hook_4, 5: hook_5, 6: hook_6},
    )
    states[BLOCKS] = state[...]
    stored.append(send.local(raw, raw_o))
    stored.append(send.local(gates, gates_o))
    stored.append(send.local(steps, steps_o))
    stored.append(send.local(scan, scan_o))
    stored.append(send.local(states, states_o))
    crossing = []
    for u in range(4):
        finish(backs[u])
        pairs = pl.ds(2 * u, 2)
        both = mm(back[pairs].reshape(L, D), out[...].reshape(D, 2 * IN)).astype(bf16)
        g_gated[pairs, place.hi] = both[:, :IN].reshape(2, L // 2, IN)
        halves[pairs] = both[:, IN:].reshape(2, L // 2, IN)
        crossing.append(send(halves.at[pairs], g_gated.at[pairs, place.hi], place.across))
    stored.append(send.local(back, back_o))

    for u in range(4):
        crossing[u].wait_recv()
        for i in (2 * u, 2 * u + 1):
            part = g_gated[i].reshape(L, IN).astype(f32) * gain[...] * mixed[pl.ds(i * L, L)]
            product = jnp.sum(part, axis=1, keepdims=True)
            squares[...] = jnp.where(lane == i + 8, product, squares[...])
    stored.append(send.local(g_gated, g_gated_o))
    inbox[place.mp] = squares[...].T[:16]
    copies = [send(inbox.at[place.mp], inbox.at[place.mp], peer) for peer in place.group]
    for copy in copies:
        copy.wait_recv()
    total = inbox[0]
    for k in range(1, GROUP):
        total = total + inbox[k]
    top = lax.rsqrt(total[:8] * (1.0 / INNER) + epsilon)
    found = jnp.concatenate([top, total[8:], jnp.zeros((112, L), f32)], 0).T
    sums[...] = found
    for i in range(BLOCKS):
        rounded = (mixed[pl.ds(i * L, L)] * found[:, i : i + 1] * gain[...]).astype(bf16)
        gated[i] = rounded.reshape(2, L // 2, IN)
    stored.append(send.local(gated, gated_o))
    for copy in stored:
        copy.wait()
    send.drain()


def back_kernel(
    whole_i, weights_i, out_i, back_i, raw_i, gates_i, steps_i, scan_i, states_i, g_gated_i, gated_i,
    sums, taps, heads, skip, gain, tokens, grad_out, valid, norm_gain,
    layer_out, token_grad, gain_grad, main_grad, side_grad, out_grad, shared_sums, copy_sums,
    weights, out, gated, gated_in, raw, gates, steps, scan, states, g_gated, g_all, left,
    row_parts, row_x, row_xx, parts, y_in, x_in, xx_in, t_out, t_in,
    grads, core_in, z_in, y_out, w_in, o_core, o_z, o_out, o_in, pair_out, pair_in,
    totals, d_state, after,
    inbox, side_box, sums_box, gain_box, gain_all, send_sem, recv_sem, local_sem,
):
    (
        whole_i, weights_i, out_i, back_i, raw_i, gates_i, steps_i, scan_i, states_i, g_gated_i,
        gated_i, sums, taps, heads, skip, gain, tokens, grad_out, valid, norm_gain, layer_out,
        token_grad, gain_grad, main_grad, side_grad, out_grad, shared_sums, copy_sums, weights,
        out, gated, gated_in, raw, gates, steps, scan, states, g_gated, g_all, left,
        row_parts, row_x, row_xx, parts, y_in, x_in, xx_in, t_out, t_in, grads, core_in,
        z_in, y_out, w_in, o_core, o_z, o_out, o_in, pair_out, pair_in, totals, d_state,
        after, inbox, side_box, sums_box, gain_box, gain_all,
    ) = map(
        View,
        (
            whole_i, weights_i, out_i, back_i, raw_i, gates_i, steps_i, scan_i, states_i, g_gated_i,
            gated_i, sums, taps, heads, skip, gain, tokens, grad_out, valid, norm_gain, layer_out,
            token_grad, gain_grad, main_grad, side_grad, out_grad, shared_sums, copy_sums, weights,
            out, gated, gated_in, raw, gates, steps, scan, states, g_gated, g_all, left,
            row_parts, row_x, row_xx, parts, y_in, x_in, xx_in, t_out, t_in, grads, core_in,
            z_in, y_out, w_in, o_core, o_z, o_out, o_in, pair_out, pair_in, totals, d_state,
            after, inbox, side_box, sums_box, gain_box, gain_all,
        ),
    )
    place = Place()
    send = Sender(send_sem, recv_sem, local_sem)

    def loads(i, slot):
        return [
            (raw_i.at[pl.ds(pl.multiple_of(i * L, 8), L + 8)], raw.at[slot]),
            (gates_i.at[rows(i)], gates.at[slot]),
            (steps_i.at[rows(i)], steps.at[slot]),
            (scan_i.at[rows(i)], scan.at[slot]),
            (states_i.at[i], states.at[slot]),
            (g_gated_i.at[i], g_gated.at[slot]),
        ]

    def load(i, slot, start):
        for k, (source, target) in enumerate(loads(i, slot)):
            copy = pltpu.make_async_copy(
                source.build(), target.build(), local_sem.at[10 + 6 * slot + k]
            )
            if start:
                copy.start()
            else:
                copy.wait()

    load(BLOCKS - 1, 1, True)
    first = [
        send.local(gated_i.at[:, place.hi], gated),
        send.local(out_i, out),
        send.local(weights_i, weights),
    ]
    load(BLOCKS - 2, 0, True)
    meet(place.group + place.copies)
    crossing = [
        send(gated_i.at[pl.ds(2 * u, 2), place.lo], gated_in.at[pl.ds(2 * u, 2)], place.across)
        for u in (3, 2, 1, 0)
    ][::-1]
    d_state[...] = jnp.zeros((N, IN), f32)
    after[...] = jnp.zeros((8, MIX), f32)
    totals[...] = jnp.zeros((8, MIX), f32)
    first[0].wait()
    first[1].wait()
    first[2].wait()

    def body(j):
        i = BLOCKS - 1 - j
        slot = lax.rem(i, 2)
        load(i, slot, False)
        g, ds, top, found = bwd_block(
            raw[slot], gates[slot], steps[slot], taps[...], heads[...], skip[...], gain[...],
            states[slot], scan[slot], pick(sums[...], i), pick(sums[...], i + 8),
            g_gated[slot].reshape(L, IN).astype(f32), d_state[...], after[...],
        )
        pl.when(i >= 2)(lambda: load(i - 2, slot, True))
        g_all[rows(i)] = g
        d_state[...] = ds
        after[...] = top
        tap_sums, gain_sum, skip_sum, decay_sum, bias_sum = found
        blank = jnp.zeros((1, MIX - IN), f32)
        fill = jnp.zeros((1, MIX - 2 * N), f32)
        totals[...] += jnp.concatenate(
            [
                tap_sums,
                jnp.concatenate([gain_sum, blank], 1),
                jnp.concatenate([skip_sum, blank], 1),
                jnp.concatenate([decay_sum, bias_sum, fill], 1),
            ],
            0,
        )
        part = mm_nt(g, weights[...].reshape(D, COLS))
        parts[i] = part.astype(bf16).reshape(GROUP, PIECE, D)

    def keep_layer(i, total):
        layer_out[i] = (tokens[i].astype(f32) + valid[i] * total).astype(bf16)

    row_units = [
        row_scatter_unit(
            send, place, row_parts, 2 * u, row_x.at[u], row_xx.at[u], keep_layer
        )
        for u in range(4)
    ]
    units = [
        scatter_unit(
            send, place, parts, 2 * u, 2 * u + 1,
            y_in.at[u], x_in.at[u], xx_in.at[u], t_out.at[u], t_in.at[u], token_grad,
        )
        for u in range(4)
    ]

    def row_product(u):
        crossing[u].wait_recv()
        pairs = pl.ds(2 * u, 2)
        own = gated[pairs].reshape(L, IN)
        other = gated_in[pairs].reshape(L, IN)
        flat = out[...].reshape(D, 2 * IN)
        part = mm_nt(own, flat[:, :IN]) + mm_nt(other, flat[:, IN:])
        row_parts[pairs] = part.astype(bf16).reshape(2, 4, PIECE, D)
        step(row_units[u])

    o_swaps, swaps = [], []
    o_grads = grads.at[:, :, :, pl.ds(0, 2 * IN)]
    back_loads = []

    def load_back(i):
        source = back_i.at[:, :, :, pl.ds(i * 384, 384)]
        back_loads.append(send.local(source, left.at[i % 2, :, pl.ds(0, 4)]))

    def out_products():
        for i in range(4):
            back_loads[i].wait()
            side = left[i % 2, :, pl.ds(0, 4)].reshape(BLOCKS * L // 2, 384)
            own = gated[...].reshape(BLOCKS * L // 2, IN)
            other = gated_in[...].reshape(BLOCKS * L // 2, IN)
            pairs = pl.ds(2 * i, 2)
            grads[pairs, :, :, :IN] = mm_tn(side, own).astype(bf16).reshape(2, 2, 96, IN)
            grads[pairs, :, :, IN : 2 * IN] = (
                mm_tn(side, other).astype(bf16).reshape(2, 2, 96, IN)
            )
            if i < 2:
                load_back(i + 2)
            o_swaps.append(
                send(o_grads.at[pairs, place.other_core], o_core.at[pairs], place.mate)
            )

    def keep_out(total):
        pair_out[...] = total[:, IN:]
        out_grad[...] = total[:, :IN]

    o_plan = reduce_steps(send, place, o_grads, o_swaps, o_core, o_z, o_out, o_in, keep_out)
    whole_loads = []

    def load_whole(i):
        source = whole_i.at[:, :, :, pl.ds(i * 384, 384)]
        whole_loads.append(send.local(source, left.at[i % 2]))

    def hook_0():
        row_product(3)

    def hook_1():
        step(units[3])
        row_product(2)
        step(row_units[3])

    def hook_2():
        step(units[3])
        row_product(1)
        step(row_units[3])
        step(row_units[2])

    def hook_3():
        step(units[2])
        step(units[3])
        row_product(0)
        step(row_units[1])
        step(row_units[2])
        load_back(0)
        load_back(1)

    def hook_4():
        step(units[3], 2)
        step(units[2])
        step(row_units[0])
        step(row_units[1])
        out_products()
        load_whole(0)
        load_whole(1)

    def hook_5():
        step(units[1])
        step(units[3], 2)
        step(units[2], 2)
        step(row_units[0])
        step(o_plan)

    def hook_6():
        step(units[1])
        step(units[2], 2)
        step(o_plan)

    crossed = []

    def hook_7():
        send.drain()
        step(units[0])
        step(units[1], 2)
        step(units[2])
        step(o_plan)
        crossed.append(send(pair_out, pair_in, place.across))

    run_blocks(
        body,
        {
            0: hook_0, 1: hook_1, 2: hook_2, 3: hook_3,
            4: hook_4, 5: hook_5, 6: hook_6, 7: hook_7,
        },
    )

    sums_box[place.dp] = totals[...]
    early = [send(sums_box.at[place.dp], sums_box.at[place.dp], peer) for peer in place.copies]

    for i in range(4):
        whole_loads[i].wait()
        side = left[i % 2].reshape(BLOCKS * L, 384)
        pairs = pl.ds(2 * i, 2)
        grads[pairs] = mm_tn(side, g_all[...]).astype(bf16).reshape(2, 2, 96, COLS)
        if i < 2:
            load_whole(i + 2)
        swaps.append(send(grads.at[pairs, place.other_core], core_in.at[pairs], place.mate))
        step(units[0])
        step(units[1])

    def keep_main(total):
        main_grad[...] = total[:, : 2 * IN]
        side_box[place.mp] = total[:, 2 * IN :].astype(bf16)

    plan = reduce_steps(send, place, grads, swaps, core_in, z_in, y_out, w_in, keep_main)
    step(plan)
    finish(units[2])
    finish(units[1])
    finish(units[0])
    crossed[0].wait_recv()
    out_grad[...] += pair_in[...]

    gain_row = norm_gain[...]
    gain_sum = jnp.zeros((1, D), f32)
    for i in range(BLOCKS):
        x = tokens[i].astype(f32)
        s = lax.rsqrt(jnp.mean(x * x, axis=1, keepdims=True) + epsilon)
        g = token_grad[i]
        dot = jnp.sum(g * gain_row * x, axis=1, keepdims=True)
        token_grad[i] = grad_out[i].astype(f32) + s * gain_row * g - x * (s * s * s * dot * (1.0 / D))
        gain_sum = gain_sum + jnp.sum(g * x * s, axis=0, keepdims=True)
    gain_box[place.mp] = jnp.concatenate([gain_sum, jnp.zeros((7, D), f32)], 0)
    gains = [send(gain_box.at[place.mp], gain_box.at[place.mp], peer) for peer in place.group]

    for copy in early:
        copy.wait_recv()
    copied = sums_box[0]
    for k in range(1, DP):
        copied = copied + sums_box[k]
    copy_sums[...] = copied
    inbox[place.mp] = copied[:, IN:]
    shares = [send(inbox.at[place.mp], inbox.at[place.mp], peer) for peer in place.group]
    step(plan)
    for copy in gains:
        copy.wait_recv()
    total = gain_box[0]
    for k in range(1, GROUP):
        total = total + gain_box[k]
    gain_all[place.dp] = total
    ends = [send(gain_all.at[place.dp], gain_all.at[place.dp], peer) for peer in place.copies]
    step(plan)
    sides = [send(side_box.at[place.mp], side_box.at[place.mp], peer) for peer in place.group]
    for copy in ends:
        copy.wait_recv()
    total = gain_all[0]
    for k in range(1, DP):
        total = total + gain_all[k]
    gain_grad[...] = total
    for copy in sides + shares:
        copy.wait_recv()
    both, steps_sum = 0.0, 0.0
    lane = lax.broadcasted_iota(jnp.int32, (N, N), 1)
    source = lax.broadcasted_iota(jnp.int32, (N, N), 0)
    shared = inbox[0]
    for k in range(GROUP):
        piece = side_box[k]
        both = both + piece[:, : 2 * N].astype(f32)
        spot = jnp.where((lane == source + HD * k) & (source < HD), 1.0, 0.0).astype(bf16)
        steps_sum = steps_sum + mm(piece[:, 2 * N :], spot)
        if k:
            shared = shared + inbox[k]
    side_grad[...] = jnp.concatenate([both, steps_sum], 1)
    shared_sums[...] = shared
    send.drain()


def call(kernel, outs, scratch, sems, collective, args, flops):
    vmem, anywhere = pltpu.VMEM, pl.ANY
    spec = {True: pl.BlockSpec(memory_space=anywhere), False: pl.BlockSpec(memory_space=vmem)}
    return pl.pallas_call(
        kernel,
        out_shape=[jax.ShapeDtypeStruct(shape, dtype) for shape, dtype, _ in outs],
        in_specs=[spec[far] for _, far in args],
        out_specs=[spec[far] for _, _, far in outs],
        scratch_shapes=[pltpu.VMEM(shape, dtype) for shape, dtype in scratch]
        + [pltpu.SemaphoreType.DMA((k,)) for k in sems],
        compiler_params=pltpu.CompilerParams(
            collective_id=collective, has_side_effects=True, vmem_limit_bytes=VMEM_BYTES
        ),
        cost_estimate=pl.CostEstimate(
            flops=flops,
            bytes_accessed=sum(a.size * a.dtype.itemsize for a, _ in args),
            transcendentals=0,
        ),
        name=kernel.__name__,
    )(*[a for a, _ in args])


def on_device(
    tokens,
    seq_len,
    norm_gain,
    main_weight,
    side_weight,
    side_terms,
    channel_terms,
    head_terms,
    output_weight,
    cotangent,
):
    place = lax.axis_index("mp")
    count, span = BLOCKS * L, D // DP
    seq = tokens[0].astype(f32)
    scale = lax.rsqrt(jnp.mean(seq * seq, axis=-1, keepdims=True) + epsilon)
    normed = (seq * scale * norm_gain).astype(bf16)
    positions = (
        jnp.arange(BLOCKS)[:, None] * L + place * PIECE + jnp.arange(PIECE)[None, :]
    )
    valid = (positions < seq_len[0]).astype(f32)[:, :, None]
    grad_branch = (valid * cotangent[0].astype(f32)).astype(bf16)
    own_steps = lax.dynamic_slice_in_dim(side_weight, 2 * N + place * HD, HD, 1)
    own_weights = jnp.concatenate(
        [
            main_weight.reshape(span, 2 * IN),
            side_weight[:, : 2 * N],
            own_steps,
            jnp.zeros((span, N - HD), bf16),
        ],
        1,
    )
    taps = jnp.concatenate([channel_terms[: CONV + 1], side_terms], 1)
    taps = jnp.concatenate([taps, jnp.zeros((3, MIX), f32)], 0)
    gain = channel_terms[CONV + 1 :]
    heads = jnp.zeros((8, N), f32)
    heads = heads.at[0, :HD].set(head_terms[0]).at[1, :HD].set(-jnp.exp(head_terms[1]))
    skip = jnp.repeat(head_terms[2], PW)[None]

    kept = [
        ((BLOCKS, GROUP, PIECE, D), bf16),
        ((DP, span, COLS), bf16),
        ((DP, span, 2 * IN), bf16),
        ((BLOCKS, 4, PIECE, D), bf16),
        ((count + 8, MIX), f32),
        ((count, IN), f32),
        ((count, N), f32),
        ((count, IN), f32),
        ((BLOCKS + 1, N, IN), f32),
        ((BLOCKS, 2, L // 2, IN), bf16),
        ((BLOCKS, 2, L // 2, IN), bf16),
    ]
    scratch = kept[:8] + [((count, IN), f32)] + kept[8:]
    scratch += [
        ((BLOCKS, L // 2, IN), bf16),
        ((L, 128), f32),
        ((N, IN), f32),
        ((GROUP, 16, L), f32),
    ]
    near = [(a, False) for a in (normed, own_weights, output_weight.T, grad_branch)]
    small = [(a, False) for a in (taps, heads, skip, gain)]
    *saved, sums = call(
        front_kernel,
        [(shape, dtype, True) for shape, dtype in kept] + [((L, 128), f32, False)],
        scratch,
        (192, 192, 16),
        0,
        near + small,
        12 * 10**9,
    )
    ends = (tokens[0], cotangent[0], valid, norm_gain[None])
    layer_out, token_grad, gain_grad, main_grad, side_grad, out_grad, shared_sums, copy_sums = call(
        back_kernel,
        [
            ((BLOCKS, PIECE, D), bf16, False),
            ((BLOCKS, PIECE, D), f32, False),
            ((8, D), f32, False),
            ((span, 2 * IN), f32, False),
            ((span, 3 * N), f32, False),
            ((span, IN), f32, False),
            ((8, 2 * N), f32, False),
            ((8, MIX), f32, False),
        ],
        [
            ((DP, span, COLS), bf16),
            ((DP, span, 2 * IN), bf16),
            ((BLOCKS, L // 2, IN), bf16),
            ((BLOCKS, L // 2, IN), bf16),
            ((2, L + 8, MIX), f32),
            ((2, L, IN), f32),
            ((2, L, N), f32),
            ((2, L, IN), f32),
            ((2, N, IN), f32),
            ((2, 2, L // 2, IN), bf16),
            ((count, COLS), bf16),
            ((2, BLOCKS, GROUP, PIECE, 384), bf16),
            ((BLOCKS, 4, PIECE, D), bf16),
            ((4, 2, PIECE, D), bf16),
            ((4, 2, 2, PIECE, D), bf16),
            ((BLOCKS, GROUP, PIECE, D), bf16),
            ((4, 4, PIECE, D), bf16),
            ((4, 3, 2, PIECE // 2, D), bf16),
            ((4, 3, 2, PIECE, D), bf16),
            ((4, PIECE, D), bf16),
            ((4, PIECE, D), bf16),
            ((8, 2, span, COLS), bf16),
            ((8, span, COLS), bf16),
            ((3, 2, span, COLS), bf16),
            ((span, COLS), bf16),
            ((span, COLS), bf16),
            ((8, span, 2 * IN), bf16),
            ((3, 2, span, 2 * IN), bf16),
            ((span, 2 * IN), bf16),
            ((span, 2 * IN), bf16),
            ((span, IN), f32),
            ((span, IN), f32),
            ((8, MIX), f32),
            ((N, IN), f32),
            ((8, MIX), f32),
            ((GROUP, 8, 2 * N), f32),
            ((GROUP, span, 3 * N), bf16),
            ((DP, 8, MIX), f32),
            ((GROUP, 8, D), f32),
            ((DP, 8, D), f32),
        ],
        (224, 224, 24),
        1,
        [(a, True) for a in saved]
        + [(sums, False)]
        + small
        + [(a, False) for a in ends],
        24 * 10**9,
    )
    main_grad = main_grad.reshape(span, 2, IN)
    conv_total = shared_sums[: CONV + 1]
    channel_total = copy_sums[: CONV + 2, :IN]
    decay = heads[1, :HD] * copy_sums[CONV + 3, :HD]
    skip_total = copy_sums[CONV + 2, :IN].reshape(HD, PW).sum(1)
    head_total = jnp.stack([copy_sums[CONV + 3, N : N + HD], decay, skip_total])
    return (
        layer_out[None],
        token_grad[None],
        gain_grad[0],
        main_grad,
        side_grad[:, : 2 * N + 48],
        conv_total,
        channel_total,
        head_total,
        out_grad.T,
    )


def solution(mesh):
    placed = (
        P("dp", None, "mp", None),
        P("dp"),
        P(),
        P("dp", None, "mp"),
        P("dp", None),
        P(),
        P(None, "mp"),
        P(None, "mp"),
        P("mp", "dp"),
        P("dp", None, "mp", None),
    )
    return jax.shard_map(
        on_device,
        mesh=mesh,
        in_specs=placed,
        out_specs=(
            P("dp", None, "mp", None),
            P("dp", None, "mp", None),
            P(),
            P("dp", None, "mp"),
            P("dp", None),
            P(),
            P(None, "mp"),
            P(None, "mp"),
            P("mp", "dp"),
        ),
        check_vma=False,
    )
```

time: 419 us -> 294 us (0.70)
  Pallas kernels: 395 us -> 267 us
    pallas_call x4 -> x2, Pallas kernels: 395 us -> 267 us  [call(): pl.pallas_call(kernel, out_shape=[jax.ShapeDtypeStruct(shape, dtype) for...]
where the time goes in v2:
time: 294 us; the launch traced here: 293 us
  Pallas kernels  267 us (91%)
  local copies, waits for them, and re-layouts  17.2 us (6%)
  other arithmetic  7.29 us (2%)
    pallas_call x2, Pallas kernels, call(): pl.pallas_call(kernel, out_shape=[jax.ShapeDtypeStruct(shape, dtype) for...  267 us
    unnamed x22, local copies, waits for them, and re-layouts  6.1 us

profile of v2, /device:TPU:1, one launch (start us, length us, event | category | flops | bytes accessed | tf_op | source)
XLA Modules:
  0.0 293.1 jit_solution(9020952113804993862)
XLA Ops:
  0.6 0.0 copy-start
  0.7 0.0 copy-start.2
  0.7 0.0 copy-start.5
  1.5 1.3 slice.80.gain
  2.7 0.8 slice_bitcast_fusion
  3.5 0.1 broadcast_in_dim.11
  3.6 0.6 broadcast_in_dim_reshape.3.skip
  4.2 0.1 scatter.9.heads
  4.3 0.0 copy-start.7
  4.4 0.1 fusion.4
  4.4 1.4 fusion
  5.8 1.3 broadcast_in_dim.24.norm_gain
  7.1 1.3 select_maximum_fusion.taps
  8.4 0.8 constant_dynamic-slice_fusion
  9.3 0.8 slice.75
  10.1 0.7 fusion.3.valid
  10.8 0.9 copy.20
  11.7 0.8 concatenate.13.own_weights
  12.5 0.0 copy-done
  12.5 0.0 copy-done.2
  12.5 0.0 copy-done.5
  12.5 1.4 fusion.2
  14.0 0.0 copy-done.7
  14.0 119.5 %front_kernel.1 = (bf16[8,8,32,1536]{3,2,1,0:T(8,128)(2,1)}, bf16[16,96,1152]{2,1,0:T(8,128)(2,1)}, bf16[16,96,768]{2,1,0:T(8,128)(2,1)}, bf16[8,4,32,1536]{3,2,...) custom-call(bf16[8,32,1536]{2,1,0:T(8,128)(2,1)} %get-tuple-element., ...), custom_call_target="tpu_custom_call" | custom-call | flops 12000000000 | bytes 1895424 | tf_op jit(solution)/shard_map/front_kernel/pallas_call | solution.py:1027
  133.5 147.5 %back_kernel.1 = (bf16[8,32,1536]{2,1,0:T(8,128)(2,1)}, f32[8,32,1536]{2,1,0:T(8,128)}, f32[8,1536]{1,0:T(8,128)}, f32[96,768]{1,0:T(8,128)}, f32[96,384]{1,0:T(...) custom-call(bf16[8,8,32,1536]{3,2,1,0:T(8,128)(2,1)} %get-tuple-element.53.whole_i, ...), custom_call_target="tpu_custom_call" | custom-call | flops 24000000000 | bytes 34592768 | tf_op jit(solution)/shard_map/back_kernel/pallas_call | solution.py:1027
  281.0 0.0 copy-start.1
  281.0 0.8 fusion.5
  281.9 0.7 slice_reduce_fusion.1
  282.6 1.3 slice.84
  283.9 0.1 reshape_squeeze.3
  284.0 0.1 reduce_sum.19
  284.1 0.6 pad_maximum_fusion
  284.7 1.4 slice_reduce_fusion
  286.1 1.8 reshape.138
  287.9 2.1 copy.28
  290.0 0.0 copy-done.1
  290.0 0.0 copy-start.4
  290.0 0.0 copy-start.6
  290.0 0.0 copy-start.3
  290.0 1.1 copy.29
  291.1 0.0 copy-done.4
  291.1 0.7 copy.30
  291.8 0.0 copy-done.6
  291.8 0.6 copy.31
  292.4 0.0 copy-done.3
  292.4 0.7 copy.32
  (4 shorter events, 0.0 us)
Async XLA Ops:
  0.6 11.9 %copy-start = (bf16[1,8,32,1536]{3,2,1,0:T(8,128)(2,1)S(1)}, bf16[1,8,32,1536]{3,2,1,0:T(8,128)(2,1)}, u32[]{:S(2)}) copy-start(bf16[1,8,32,1536]{3,2,1,0:T(8,128)(2,1)} %param.14) | copy-start | bytes 2359300
  0.7 11.9 %copy-start.2 = (bf16[1,8,32,1536]{3,2,1,0:T(8,128)(2,1)S(1)}, bf16[1,8,32,1536]{3,2,1,0:T(8,128)(2,1)}, u32[]{:S(2)}) copy-start(bf16[1,8,32,1536]{3,2,1,0:T(8,128)(2,1)} %param.23) | copy-start | bytes 2359300
  0.7 11.9 %copy-start.5 = (f32[1536]{0:T(1024)S(1)}, f32[1536]{0:T(1024)}, u32[]{:S(2)}) copy-start(f32[1536]{0:T(1024)} %param.16) | copy-start | bytes 18436
  4.3 9.6 %copy-start.7 = (f32[8,128]{1,0:T(8,128)}, f32[8,128]{1,0:T(8,128)S(1)}, u32[]{:S(2)}) copy-start(f32[8,128]{1,0:T(8,128)S(1)} %scatter.9.heads) | copy-start | bytes 12292
  281.0 9.0 %copy-start.1 = (f32[8,32,1536]{2,1,0:T(8,128)S(1)}, f32[8,32,1536]{2,1,0:T(8,128)}, u32[]{:S(2)}) copy-start(f32[8,32,1536]{2,1,0:T(8,128)} %get-tuple-element.66) | copy-start | bytes 4718596
  290.0 1.2 copy-start.4
  290.0 1.8 copy-start.6
  290.0 2.4 copy-start.3
